TPU v7x, 512 devices: a whole 4x8x8 slice. The times are simulated.
512 devices in a mesh: tile: 64 (over y_lo, z, x), head: 8 (over y_hi, core).
Axes of the slice: x: 4, y: 8 (y_hi: 4, y_lo: 2; y = y_hi * 2 + y_lo), z: 8, core: 2. Of those that a mesh axis runs over, the one named last changes fastest.
Arguments:
- q_video: bfloat16 [49152, 3072], P('tile', 'head'), may hold values from -12 to 12
- k_video: bfloat16 [49152, 3072], P('tile', 'head'), may hold values from -12 to 12
- v_video: bfloat16 [49152, 3072], P('tile', 'head'), may hold values from -6 to 6
- q_text: bfloat16 [256, 3072], P('tile', 'head'), may hold values from -12 to 12
- k_text: bfloat16 [256, 3072], P('tile', 'head'), may hold values from -6 to 6
- v_text: bfloat16 [256, 3072], P('tile', 'head'), may hold values from -6 to 6
- tile_lists: int32 [128, 8], P('tile'), may hold values from -1 to 127, as said below
- text_len: int32 [1], replicated, may hold values from 64 to 256
Outputs:
- video_out: bfloat16 [49152, 3072], P(('tile', 'head'))
- text_out: bfloat16 [256, 3072], P('tile', 'head')
Inputs may be any that keep to these rules, and one draw needn't show every extreme that they name: `tile_lists`: row g lists key tiles for video tile g, whose time, height and width tile coordinates are g % 2, (g // 2) // 8 and (g // 2) % 8; a tile's number is ((height * 8) + width) * 2 + time. The first entry is g itself, the next entries are distinct tiles whose three coordinates each differ from g's by at most one, and -1 fills the empty slots at the end. Some row is full.
All inputs are finite; a program needn't handle non-finite values.
Results may differ from a plain program's by a relative error of at most 0.0054.
Values may be sent and summed in bfloat16 or wider, within the bound.
No kernel may reach another device: no remote copies, remote signals or barrier semaphores. Data moves between devices by JAX's collectives and lax.ppermute only.
A program may use at most 128 MiB of HBM per device.

v0:
```python
import math

import jax
import jax.numpy as jnp
from jax import lax
from jax.sharding import PartitionSpec as P

HEAD_DIM = 128
TILES_W = 8


def shifted(value, axis, steps):
    count = lax.axis_size(axis)
    leading, last = (max(0, -steps), min(count, count - steps))
    return lax.ppermute(value, axis, [(source, source + steps) for source in range(leading, last)])


def absorb(state, scores, live, values, form):
    peak, total, summed = state
    scores = jnp.where(live, scores, -jnp.inf)
    new_peak = jnp.maximum(peak, jnp.max(scores, axis=-1))
    factor = jnp.exp(peak - new_peak)
    unrounded = jnp.exp(scores - new_peak[..., None])
    new_total = total * factor + jnp.sum(unrounded, axis=-1)
    update = jnp.einsum(
        form, unrounded.astype(jnp.bfloat16), values, preferred_element_type=jnp.float32
    )
    return (new_peak, new_total, summed * factor[..., None] + update)


def send_near(pair, offset):
    return shifted((pair[0], pair[1]), "tile", offset)


def shards(q_video, k_video, v_video, q_text, k_text, v_text, tile_lists, text_len):
    tiles_here = tile_lists.shape[0]
    slot_count = tile_lists.shape[1]
    rows = q_video.shape[0]
    tile_rows = rows // tiles_here
    width = q_video.shape[1]
    head_count = width // HEAD_DIM
    scale = 1.0 / math.sqrt(HEAD_DIM)
    place = lax.axis_index("tile")
    my_height = place // TILES_W
    my_width = place % TILES_W
    own_keys = k_video.reshape(tiles_here, tile_rows, width)
    own_values = v_video.reshape(tiles_here, tile_rows, width)
    key_blocks = []
    value_blocks = []
    for step_h in (-1, 0, 1):
        for step_w in (-1, 0, 1):
            if step_h == 0 and step_w == 0:
                key_blocks.append(own_keys)
                value_blocks.append(own_values)
            else:
                moved = send_near((own_keys, own_values), -(step_h * TILES_W + step_w))
                key_blocks.append(moved[0])
                value_blocks.append(moved[1])
    key_pool = jnp.concatenate(key_blocks, 0)
    value_pool = jnp.concatenate(value_blocks, 0)
    key_pool = key_pool.reshape(-1, tile_rows, head_count, HEAD_DIM)
    value_pool = value_pool.reshape(-1, tile_rows, head_count, HEAD_DIM)
    listed = tile_lists >= 0
    safe = jnp.maximum(tile_lists, 0)
    source = safe // tiles_here
    offset_h = source // TILES_W - my_height
    offset_w = source % TILES_W - my_width
    candidate = ((offset_h + 1) * 3 + offset_w + 1) * tiles_here + safe % tiles_here
    candidate = jnp.where(listed, candidate, 0)
    words = (
        lax.all_gather(q_text, "tile", axis=0, tiled=True),
        lax.all_gather(k_text, "tile", axis=0, tiled=True),
        lax.all_gather(v_text, "tile", axis=0, tiled=True),
    )
    text_total = words[0].shape[0]
    all_queries = words[0].reshape(text_total, head_count, HEAD_DIM)
    word_keys = words[1].reshape(text_total, head_count, HEAD_DIM)
    word_values = words[2].reshape(text_total, head_count, HEAD_DIM)
    text_live = jnp.arange(text_total) < text_len[0]
    queries = q_video.reshape(tiles_here, tile_rows, head_count, HEAD_DIM)
    start_state = (
        jnp.full((tiles_here, head_count, tile_rows), -jnp.inf, jnp.float32),
        jnp.zeros((tiles_here, head_count, tile_rows), jnp.float32),
        jnp.zeros((tiles_here, head_count, tile_rows, HEAD_DIM), jnp.float32),
    )

    def one_slot(slot, state):
        picked = candidate[:, slot]
        keys = jnp.take(key_pool, picked, axis=0)
        values = jnp.take(value_pool, picked, axis=0)
        scores = (
            jnp.einsum("tqhd,tkhd->thqk", queries, keys, preferred_element_type=jnp.float32) * scale
        )
        live = listed[:, slot][:, None, None, None]
        return absorb(state, scores, live, values, "thqk,tkhd->thqd")

    state = lax.fori_loop(0, slot_count, one_slot, start_state)
    word_scores = (
        jnp.einsum("tqhd,khd->thqk", queries, word_keys, preferred_element_type=jnp.float32) * scale
    )
    state = absorb(
        state, word_scores, text_live[None, None, None, :], word_values, "thqk,khd->thqd"
    )
    video_heads = state[2] / state[1][..., None]
    video_heads = jnp.transpose(video_heads, (0, 2, 1, 3)).reshape(rows, width).astype(jnp.bfloat16)
    video_out = lax.all_to_all(video_heads, "head", split_axis=0, concat_axis=1, tiled=True)
    text_here = q_text.shape[0]
    video_keys = k_video.reshape(rows, head_count, HEAD_DIM)
    video_values = v_video.reshape(rows, head_count, HEAD_DIM)
    text_scores = (
        jnp.einsum("qhd,khd->qhk", all_queries, video_keys, preferred_element_type=jnp.float32)
        * scale
    )
    local_peak = jnp.max(text_scores, axis=-1)
    unrounded = jnp.exp(text_scores - local_peak[..., None])
    local_total = jnp.sum(unrounded, axis=-1)
    local_sum = jnp.einsum(
        "qhk,khd->qhd",
        unrounded.astype(jnp.bfloat16),
        video_values,
        preferred_element_type=jnp.float32,
    )
    arrived = (
        lax.all_to_all(local_peak[None], "tile", split_axis=1, concat_axis=0, tiled=True),
        lax.all_to_all(local_total[None], "tile", split_axis=1, concat_axis=0, tiled=True),
        lax.all_to_all(local_sum[None], "tile", split_axis=1, concat_axis=0, tiled=True),
    )
    peers_peak, peers_total, peers_sum = arrived
    best_peak = jnp.max(peers_peak, axis=0)
    factors = jnp.exp(peers_peak - best_peak[None])
    own_state = (
        best_peak,
        jnp.sum(peers_total * factors, axis=0),
        jnp.sum(peers_sum * factors[..., None], axis=0),
    )
    own_queries = q_text.reshape(text_here, head_count, HEAD_DIM)
    own_scores = (
        jnp.einsum("qhd,khd->qhk", own_queries, word_keys, preferred_element_type=jnp.float32)
        * scale
    )
    own_state = absorb(own_state, own_scores, text_live[None, None, :], word_values, "qhk,khd->qhd")
    text_out = (
        (own_state[2] / own_state[1][..., None]).reshape(text_here, width).astype(jnp.bfloat16)
    )
    return (video_out, text_out)


def solution(mesh):
    in_specs = (
        P("tile", "head"),
        P("tile", "head"),
        P("tile", "head"),
        P("tile", "head"),
        P("tile", "head"),
        P("tile", "head"),
        P("tile", None),
        P(),
    )
    out_specs = (P(("tile", "head"), None), P("tile", "head"))
    return jax.shard_map(shards, mesh=mesh, in_specs=in_specs, out_specs=out_specs, check_vma=False)
```

profile of v0, /device:TPU:8, one launch (start us, length us, event | category | flops | bytes accessed | tf_op | source)
XLA Modules:
  0.0 972.9 jit_solution(13735697652264501117)
XLA Ops:
  0.6 7.0 collective-permute-start
  7.7 7.3 collective-permute-start.1
  15.0 5.5 collective-permute-start.2
  20.5 2.2 collective-permute-start.3
  22.7 7.9 collective-permute-start.4
  31.8 226.1 %all-gather.2 = bf16[64,4,384]{2,1,0:T(4,128)(2,1)S(1)} all-gather(bf16[1,4,384]{2,1,0:T(4,128)(2,1)} %bitcast.158), channel_id=1, replica_groups=mesh['tile'=64,'head'=8] {'tile'}, dimensions={0}, use_global_device_ids=true | all-gather | bytes 199680 | tf_op jit(solution)/shard_map/all_gather | solution.py:71
  259.4 5.9 all-to-all-start.2
  265.3 2.0 reshape.166
  267.3 2.6 reshape.167
  269.9 2.1 copy.253
  274.0 2.2 copy.235
  276.1 2.2 copy.225
  278.3 1.8 reshape.125
  282.6 171.6 %all-gather = bf16[64,4,384]{2,1,0:T(4,128)(2,1)} all-gather(bf16[1,4,384]{2,1,0:T(4,128)(2,1)} %bitcast.156), channel_id=1, replica_groups=mesh['tile'=64,'head'=8] {'tile'}, dimensions={0}, use_global_device_ids=true | all-gather | bytes 199680 | tf_op jit(solution)/shard_map/all_gather | solution.py:72
  459.7 2.1 collective-permute-start.5
  461.7 1.9 collective-permute-start.6
  463.7 3.8 collective-permute-start.7
  468.7 3.5 bitcast_reduce_fusion.2
  472.1 3.9 collective-permute-start.8
  476.1 185.6 %all-gather.1 = bf16[64,4,384]{2,1,0:T(4,128)(2,1)S(1)} all-gather(bf16[1,4,384]{2,1,0:T(4,128)(2,1)S(1)} %bitcast.157), channel_id=1, replica_groups=mesh['tile'=64,'head'=8] {'tile'}, dimensions={0}, use_global_device_ids=true | all-gather | bytes 199680 | tf_op jit(solution)/shard_map/all_gather | solution.py:73
  670.0 1.9 collective-permute-start.9
  673.3 1.9 collective-permute-start.10
  675.2 2.1 copy.221
  678.1 1.9 collective-permute-start.11
  681.5 8.1 collective-permute-start.12
  689.6 2.1 copy.223
  695.4 3.6 collective-permute-start.13
  701.7 5.0 collective-permute-start.14
  708.5 12.2 %copy.236 = bf16[18,384,3,128]{3,2,1,0:T(4,128)(2,1)} copy(bf16[18,384,3,128]{1,3,2,0:T(8,128)(2,1)} %constant_dynamic-update-slice_fusion) | data formatting | bytes 10616832
  723.4 2.6 collective-permute-start.15
  742.7 12.2 %copy.238 = bf16[18,384,3,128]{3,2,1,0:T(4,128)(2,1)} copy(bf16[18,384,3,128]{1,3,2,0:T(8,128)(2,1)} %constant_dynamic-update-slice_fusion.9) | data formatting | bytes 10616832
  754.9 150.2 %while.18 = (s32[]{:T(128)}, f32[2,3,384]{2,1,0:T(4,128)S(1)}, f32[2,3,384]{2,1,0:T(4,128)}, f32[2,3,384,128]{3,2,1,0:T(8,128)}, pred[2,8]{0,1:T(8,128)(4,1)}, /...) while((s32[]{:T(128)}, f32[2,3,384]{2,1,0:T(4,128)S(1)}, ...), condition=%wide.region_3.5_spmd.clone, body=%wide.region_0.4_spmd.clone.sunk | while | flops 464204032 | bytes 31486276 | solution.py:97
  755.6 4.3 gather_fusion
  759.9 4.3 gather_fusion.1
  766.5 2.3 bitcast_reduce_fusion.4
  774.4 4.3 gather_fusion
  778.7 4.3 gather_fusion.1
  785.3 2.3 bitcast_reduce_fusion.4
  793.2 4.3 gather_fusion
  797.4 4.3 gather_fusion.1
  804.1 2.3 bitcast_reduce_fusion.4
  811.9 4.3 gather_fusion
  816.2 4.3 gather_fusion.1
  822.8 2.3 bitcast_reduce_fusion.4
  830.7 4.3 gather_fusion
  835.0 4.3 gather_fusion.1
  841.6 2.3 bitcast_reduce_fusion.4
  849.5 4.3 gather_fusion
  853.8 4.3 gather_fusion.1
  860.4 2.3 bitcast_reduce_fusion.4
  868.2 4.3 gather_fusion
  872.5 4.3 gather_fusion.1
  879.1 2.3 bitcast_reduce_fusion.4
  887.0 4.3 gather_fusion
  891.3 4.3 gather_fusion.1
  897.9 2.3 bitcast_reduce_fusion.4
  905.1 13.8 %all-to-all-start.3 = ((f32[1,256,3]{2,0,1:T(1,128)}), f32[1,256,3]{2,0,1:T(1,128)S(1)}, u32[]{:S(2)}, u32[]{:S(2)}) async-start(f32[1,256,3]{2,0,1:T(1,128)} %copy.264), calls=%async_computation.3 | async-start | bytes 262144 | tf_op jit(solution)/shard_map/all_to_all | solution.py:125
  919.6 8.8 all-to-all-done.3
  928.4 5.9 all-to-all-start.1
  934.3 2.2 fusion.22
  937.3 3.4 fusion.27
  942.4 3.4 all-to-all-done.1
  945.9 7.1 all-to-all-start
  957.6 14.4 %all-to-all-done = bf16[8,96,384]{2,1,0:T(8,128)(2,1)S(1)} async-done(((bf16[8,96,384]{2,1,0:T(8,128)(2,1)}), bf16[8,96,384]{2,1,0:T(8,128)(2,1)S(1)}, u32[]{:S(2)}, u32[]{:S(2)}) %all-to-all-start) | async-done | bytes 589856 | tf_op jit(solution)/shard_map/all_to_all | solution.py:106
  (267 shorter events, 124.0 us)
Async XLA Ops:
  0.6 459.0 %collective-permute-start = (bf16[2,384,384]{2,1,0:T(8,128)(2,1)}, bf16[2,384,384]{2,1,0:T(8,128)(2,1)}, u32[]{:S(2)}, u32[]{:S(2)}) collective-permute-start(bf16[2,384,384]{2,1,0:T(8,128)(2,1)} %bitcast.140), channel_id=1, source_target_pairs={{0,72},{8,80},{16,88},{24,96},{32,104},{40,112},{48,120},{56,128},... | collective-permute-start | bytes 1769480 | tf_op jit(solution)/shard_map/ppermute | solution.py:15
  7.7 454.1 %collective-permute-start.1 = (bf16[2,384,384]{2,1,0:T(8,128)(2,1)}, bf16[2,384,384]{2,1,0:T(8,128)(2,1)}, u32[]{:S(2)}, u32[]{:S(2)}) collective-permute-start(bf16[2,384,384]{2,1,0:T(8,128)(2,1)} %bitcast.141), channel_id=1, source_target_pairs={{0,64},{8,72},{16,80},{24,88},{32,96},{40,104},{48,112},{56,120},{... | collective-permute-start | bytes 1769480 | tf_op jit(solution)/shard_map/ppermute | solution.py:15
  15.0 448.7 %collective-permute-start.2 = (bf16[2,384,384]{2,1,0:T(8,128)(2,1)}, bf16[2,384,384]{2,1,0:T(8,128)(2,1)}, u32[]{:S(2)}, u32[]{:S(2)}) collective-permute-start(bf16[2,384,384]{2,1,0:T(8,128)(2,1)} %bitcast.142), channel_id=1, source_target_pairs={{0,56},{8,64},{16,72},{24,80},{32,88},{40,96},{48,104},{56,112},{6... | collective-permute-start | bytes 1769480 | tf_op jit(solution)/shard_map/ppermute | solution.py:15
  20.5 451.7 %collective-permute-start.3 = (bf16[2,384,384]{2,1,0:T(8,128)(2,1)}, bf16[2,384,384]{2,1,0:T(8,128)(2,1)}, u32[]{:S(2)}, u32[]{:S(2)}) collective-permute-start(bf16[2,384,384]{2,1,0:T(8,128)(2,1)} %bitcast.143), channel_id=1, source_target_pairs={{0,8},{8,16},{16,24},{24,32},{32,40},{40,48},{48,56},{56,64},{64,7... | collective-permute-start | bytes 1769480 | tf_op jit(solution)/shard_map/ppermute | solution.py:15
  22.7 647.3 %collective-permute-start.4 = (bf16[2,384,384]{2,1,0:T(8,128)(2,1)}, bf16[2,384,384]{2,1,0:T(8,128)(2,1)}, u32[]{:S(2)}, u32[]{:S(2)}) collective-permute-start(bf16[2,384,384]{2,1,0:T(8,128)(2,1)} %bitcast.144), channel_id=1, source_target_pairs={{8,0},{16,8},{24,16},{32,24},{40,32},{48,40},{56,48},{64,56},{72,6... | collective-permute-start | bytes 1769480 | tf_op jit(solution)/shard_map/ppermute | solution.py:15
  258.0 14.0 %copy-start.17 = (s32[2,8]{1,0:T(2,128)S(1)}, s32[2,8]{1,0:T(2,128)}, u32[]{:S(2)}) copy-start(s32[2,8]{1,0:T(2,128)} %param.18) | copy-start | bytes 196
  259.4 645.7 %all-to-all-start.2 = ((f32[1,256,3]{2,0,1:T(1,128)}), f32[1,256,3]{2,0,1:T(1,128)}, u32[]{:S(2)}, u32[]{:S(2)}) async-start(f32[1,256,3]{2,0,1:T(1,128)} %copy.258), calls=%async_computation.2 | async-start | bytes 262144 | tf_op jit(solution)/shard_map/all_to_all | solution.py:124
  276.1 182.1 %copy-start.1 = (bf16[768,384]{0,1:T(8,128)(2,1)S(1)}, bf16[768,384]{0,1:T(8,128)(2,1)}, u32[]{:S(2)}) copy-start(bf16[768,384]{0,1:T(8,128)(2,1)} %copy.253) | copy-start | bytes 1769476
  456.9 19.1 %copy-start.13 = (bf16[4,384]{1,0:T(4,128)(2,1)S(1)}, bf16[4,384]{1,0:T(4,128)(2,1)}, u32[]{:S(2)}) copy-start(bf16[4,384]{1,0:T(4,128)(2,1)} %param.17) | copy-start | bytes 9220
  459.6 202.9 %copy-start.12 = (f32[256,3]{0,1:T(4,128)S(1)}, f32[256,3]{0,1:T(4,128)}, u32[]{:S(2)}) copy-start(f32[256,3]{0,1:T(4,128)} %fusion.20) | copy-start | bytes 9220
  459.6 203.7 %copy-start.6 = (f32[1,256,3,128]{3,1,2,0:T(8,128)S(1)}, f32[1,256,3,128]{3,1,2,0:T(8,128)}, u32[]{:S(2)}) copy-start(f32[1,256,3,128]{3,1,2,0:T(8,128)} %convolution_bitcast_fusion.1) | copy-start | bytes 1179652
  459.6 16.4 %copy-start.15 = (pred[256]{0:T(512)(128)(4,1)}, pred[256]{0:T(512)(128)(4,1)S(1)}, u32[]{:S(2)}) copy-start(pred[256]{0:T(512)(128)(4,1)S(1)} %iota_compare_fusion) | copy-start | bytes 772
  459.7 213.6 %collective-permute-start.5 = (bf16[2,384,384]{2,1,0:T(8,128)(2,1)}, bf16[2,384,384]{2,1,0:T(8,128)(2,1)}, u32[]{:S(2)}, u32[]{:S(2)}) collective-permute-start(bf16[2,384,384]{2,1,0:T(8,128)(2,1)} %bitcast.145), channel_id=1, source_target_pairs={{56,0},{64,8},{72,16},{80,24},{88,32},{96,40},{104,48},{112,56},{1... | collective-permute-start | bytes 1769480 | tf_op jit(solution)/shard_map/ppermute | solution.py:15
  461.7 215.6 %collective-permute-start.6 = (bf16[2,384,384]{2,1,0:T(8,128)(2,1)}, bf16[2,384,384]{2,1,0:T(8,128)(2,1)S(1)}, u32[]{:S(2)}, u32[]{:S(2)}) collective-permute-start(bf16[2,384,384]{2,1,0:T(8,128)(2,1)} %bitcast.146), channel_id=1, source_target_pairs={{64,0},{72,8},{80,16},{88,24},{96,32},{104,40},{112,48},{120,56},{... | collective-permute-start | bytes 1769480 | tf_op jit(solution)/shard_map/ppermute | solution.py:15
  463.7 217.8 %collective-permute-start.7 = (bf16[2,384,384]{2,1,0:T(8,128)(2,1)}, bf16[2,384,384]{2,1,0:T(8,128)(2,1)}, u32[]{:S(2)}, u32[]{:S(2)}) collective-permute-start(bf16[2,384,384]{2,1,0:T(8,128)(2,1)} %bitcast.147), channel_id=1, source_target_pairs={{72,0},{80,8},{88,16},{96,24},{104,32},{112,40},{120,48},{128,56},... | collective-permute-start | bytes 1769480 | tf_op jit(solution)/shard_map/ppermute | solution.py:15
  472.1 223.2 %collective-permute-start.8 = (bf16[2,384,384]{2,1,0:T(8,128)(2,1)}, bf16[2,384,384]{2,1,0:T(8,128)(2,1)}, u32[]{:S(2)}, u32[]{:S(2)}) collective-permute-start(bf16[2,384,384]{2,1,0:T(8,128)(2,1)} %bitcast.9), channel_id=1, source_target_pairs={{0,72},{8,80},{16,88},{24,96},{32,104},{40,112},{48,120},{56,128},... | collective-permute-start | bytes 1769480 | tf_op jit(solution)/shard_map/ppermute | solution.py:15
  670.0 31.7 %collective-permute-start.9 = (bf16[2,384,384]{2,1,0:T(8,128)(2,1)}, bf16[2,384,384]{2,1,0:T(8,128)(2,1)}, u32[]{:S(2)}, u32[]{:S(2)}) collective-permute-start(bf16[2,384,384]{2,1,0:T(8,128)(2,1)} %bitcast.9), channel_id=1, source_target_pairs={{0,64},{8,72},{16,80},{24,88},{32,96},{40,104},{48,112},{56,120},{... | collective-permute-start | bytes 1769480 | tf_op jit(solution)/shard_map/ppermute | solution.py:15
  673.3 50.1 %collective-permute-start.10 = (bf16[2,384,384]{2,1,0:T(8,128)(2,1)}, bf16[2,384,384]{2,1,0:T(8,128)(2,1)}, u32[]{:S(2)}, u32[]{:S(2)}) collective-permute-start(bf16[2,384,384]{2,1,0:T(8,128)(2,1)} %bitcast.9), channel_id=1, source_target_pairs={{0,56},{8,64},{16,72},{24,80},{32,88},{40,96},{48,104},{56,112},{6... | collective-permute-start | bytes 1769480 | tf_op jit(solution)/shard_map/ppermute | solution.py:15
  678.1 49.3 %collective-permute-start.11 = (bf16[2,384,384]{2,1,0:T(8,128)(2,1)}, bf16[2,384,384]{2,1,0:T(8,128)(2,1)}, u32[]{:S(2)}, u32[]{:S(2)}) collective-permute-start(bf16[2,384,384]{2,1,0:T(8,128)(2,1)} %bitcast.9), channel_id=1, source_target_pairs={{0,8},{8,16},{16,24},{24,32},{32,40},{40,48},{48,56},{56,64},{64,7... | collective-permute-start | bytes 1769480 | tf_op jit(solution)/shard_map/ppermute | solution.py:15
  681.5 47.4 %collective-permute-start.12 = (bf16[2,384,384]{2,1,0:T(8,128)(2,1)}, bf16[2,384,384]{2,1,0:T(8,128)(2,1)}, u32[]{:S(2)}, u32[]{:S(2)}) collective-permute-start(bf16[2,384,384]{2,1,0:T(8,128)(2,1)} %bitcast.9), channel_id=1, source_target_pairs={{8,0},{16,8},{24,16},{32,24},{40,32},{48,40},{56,48},{64,56},{72,6... | collective-permute-start | bytes 1769480 | tf_op jit(solution)/shard_map/ppermute | solution.py:15
  691.7 7.2 copy-start.5
  691.7 9.1 copy-start.2
  693.6 14.0 %copy-start.3 = (bf16[2,384,384]{1,2,0:T(8,128)(2,1)S(1)}, bf16[2,384,384]{1,2,0:T(8,128)(2,1)}, u32[]{:S(2)}) copy-start(bf16[2,384,384]{1,2,0:T(8,128)(2,1)} %copy.223) | copy-start | bytes 1769476
  695.4 34.8 %collective-permute-start.13 = (bf16[2,384,384]{2,1,0:T(8,128)(2,1)}, bf16[2,384,384]{2,1,0:T(8,128)(2,1)}, u32[]{:S(2)}, u32[]{:S(2)}) collective-permute-start(bf16[2,384,384]{2,1,0:T(8,128)(2,1)} %bitcast.9), channel_id=1, source_target_pairs={{56,0},{64,8},{72,16},{80,24},{88,32},{96,40},{104,48},{112,56},{1... | collective-permute-start | bytes 1769480 | tf_op jit(solution)/shard_map/ppermute | solution.py:15
  701.7 32.6 %collective-permute-start.14 = (bf16[2,384,384]{2,1,0:T(8,128)(2,1)}, bf16[2,384,384]{2,1,0:T(8,128)(2,1)}, u32[]{:S(2)}, u32[]{:S(2)}) collective-permute-start(bf16[2,384,384]{2,1,0:T(8,128)(2,1)} %bitcast.9), channel_id=1, source_target_pairs={{64,0},{72,8},{80,16},{88,24},{96,32},{104,40},{112,48},{120,56},{... | collective-permute-start | bytes 1769480 | tf_op jit(solution)/shard_map/ppermute | solution.py:15
  723.4 17.0 %collective-permute-start.15 = (bf16[2,384,384]{2,1,0:T(8,128)(2,1)}, bf16[2,384,384]{2,1,0:T(8,128)(2,1)}, u32[]{:S(2)}, u32[]{:S(2)}) collective-permute-start(bf16[2,384,384]{2,1,0:T(8,128)(2,1)} %bitcast.9), channel_id=1, source_target_pairs={{72,0},{80,8},{88,16},{96,24},{104,32},{112,40},{120,48},{128,56},... | collective-permute-start | bytes 1769480 | tf_op jit(solution)/shard_map/ppermute | solution.py:15
  733.4 3.2 copy-start.4
  768.8 1.6 copy-start.9
  768.8 2.3 copy-start
  768.8 2.3 copy-start.18
  772.6 1.1 copy-start.19
  787.6 1.6 copy-start.9
  787.6 2.3 copy-start
  787.6 2.3 copy-start.18
  791.4 1.1 copy-start.19
  806.4 1.6 copy-start.9
  806.4 2.3 copy-start
  806.4 2.3 copy-start.18
  810.2 1.1 copy-start.19
  825.1 1.6 copy-start.9
  825.1 2.3 copy-start
  825.1 2.3 copy-start.18
  828.9 1.1 copy-start.19
  843.9 1.6 copy-start.9
  843.9 2.3 copy-start
  843.9 2.3 copy-start.18
  847.7 1.1 copy-start.19
  862.7 1.6 copy-start.9
  862.7 2.3 copy-start
  862.7 2.3 copy-start.18
  866.5 1.1 copy-start.19
  881.5 1.6 copy-start.9
  881.5 2.3 copy-start
  881.5 2.3 copy-start.18
  900.2 1.6 copy-start.9
  900.2 2.3 copy-start
  900.2 2.3 copy-start.18
  905.1 23.3 %all-to-all-start.3 = ((f32[1,256,3]{2,0,1:T(1,128)}), f32[1,256,3]{2,0,1:T(1,128)S(1)}, u32[]{:S(2)}, u32[]{:S(2)}) async-start(f32[1,256,3]{2,0,1:T(1,128)} %copy.264), calls=%async_computation.3 | async-start | bytes 262144 | tf_op jit(solution)/shard_map/all_to_all | solution.py:125
  928.4 17.5 %all-to-all-start.1 = ((f32[1,256,3,128]{3,0,2,1:T(1,128)}), f32[1,256,3,128]{3,0,2,1:T(1,128)S(1)}, u32[]{:S(2)}, u32[]{:S(2)}) async-start(f32[1,256,3,128]{3,0,2,1:T(1,128)} %copy.256), calls=%async_computation.1 | async-start | bytes 786432 | tf_op jit(solution)/shard_map/all_to_all | solution.py:126
  940.6 12.4 %copy-start.7 = (bf16[256,3,128]{2,1,0:T(4,128)(2,1)S(1)}, bf16[256,3,128]{2,1,0:T(4,128)(2,1)}, u32[]{:S(2)}) copy-start(bf16[256,3,128]{2,1,0:T(4,128)(2,1)} %reshape.127) | copy-start | bytes 589828
  940.6 12.4 %copy-start.14 = (bf16[4,384]{1,0:T(4,128)(2,1)S(1)}, bf16[4,384]{1,0:T(4,128)(2,1)}, u32[]{:S(2)}) copy-start(bf16[4,384]{1,0:T(4,128)(2,1)} %param.15) | copy-start | bytes 9220
  940.6 12.4 %copy-start.16 = (pred[256]{0:T(512)(128)(4,1)S(1)}, pred[256]{0:T(512)(128)(4,1)}, u32[]{:S(2)}) copy-start(pred[256]{0:T(512)(128)(4,1)} %copy-done.15) | copy-start | bytes 772
  940.6 16.2 %copy-start.11 = (bf16[256,3,128]{2,1,0:T(4,128)(2,1)S(1)}, bf16[256,3,128]{2,1,0:T(4,128)(2,1)}, u32[]{:S(2)}) copy-start(bf16[256,3,128]{2,1,0:T(4,128)(2,1)} %reshape.128) | copy-start | bytes 589828
  945.9 26.2 %all-to-all-start = ((bf16[8,96,384]{2,1,0:T(8,128)(2,1)}), bf16[8,96,384]{2,1,0:T(8,128)(2,1)S(1)}, u32[]{:S(2)}, u32[]{:S(2)}) async-start(bf16[8,96,384]{2,1,0:T(8,128)(2,1)} %reshape.168), calls=%async_computation | async-start | bytes 1179648 | tf_op jit(solution)/shard_map/all_to_all | solution.py:106
  (11 other events, 7.7 us)
where the time goes:
time: 977 us; the launch traced here: 973 us
  blocking collectives  583 us (60%)
  local copies, waits for them, and re-layouts  180 us (18%)
  starting transfers between devices  99.2 us (10%)
  other arithmetic  40.7 us (4%)
  matrix products  40.4 us (4%)
  waiting for transfers between devices  27 us (3%)
    all_gather x1, blocking collectives, shards(): lax.all_gather(q_text, 'tile', axis=0, tiled=True)  226 us
    all_gather x1, blocking collectives, shards(): lax.all_gather(v_text, 'tile', axis=0, tiled=True)  186 us
    all_gather x1, blocking collectives, shards(): lax.all_gather(k_text, 'tile', axis=0, tiled=True)  172 us
    ppermute x16, starting transfers between devices, shifted(): lax.ppermute(value, axis, [(source, source + steps) for source in range(l...  66.6 us
    unnamed x54, local copies, waits for them, and re-layouts  47.8 us
    gather x8, local copies, waits for them, and re-layouts, one_slot(): keys = jnp.take(key_pool, picked, axis=0)  34.2 us
    gather x8, local copies, waits for them, and re-layouts, one_slot(): values = jnp.take(value_pool, picked, axis=0)  34.2 us
    ppermute x16, local copies, waits for them, and re-layouts, shifted(): lax.ppermute(value, axis, [(source, source + steps) for source in range(l...  23.5 us
  transfers between devices with their start and end apart: 20, of which 4 were waited for; matrix products, arithmetic and copies ran while one was open for 25% of the time, Pallas kernels for 0%

commit v1 on v0

v1 whole, which is shorter than its diff:
```python
import functools
import math

import jax
import jax.numpy as jnp
import numpy as np
from jax import lax
from jax.experimental import pallas as pl
from jax.experimental.pallas import tpu as pltpu
from jax.sharding import Mesh
from jax.sharding import PartitionSpec as P


SIZES = (2, 8, 4, 4, 2)
NAMES = ("yl", "z", "x", "yh", "c")
GROUP = ("yl", "x", "c")
HEAD = 128
TILE = 384
ROWS = 2 * TILE
SLOTS = 8
BLOCK = 2 * ROWS + 16
PIECE = ROWS + 16
RATE = math.log2(math.e) / math.sqrt(HEAD)
VMEM = 40 * 1024 * 1024
CALLS = ((0, 1), (2,), (3,))
COST = pl.CostEstimate(flops=1 << 20, bytes_accessed=1 << 16, transcendentals=0)


def pairs_of(target):
    found = []
    for source in np.ndindex(*SIZES):
        aim = target(*source)
        if aim is not None:
            found.append(
                (int(np.ravel_multi_index(source, SIZES)), int(np.ravel_multi_index(aim, SIZES)))
            )
    return found


def send(value, target):
    return lax.ppermute(value, NAMES, pairs_of(target))


def to_column(turn):
    def target(yl, z, x, yh, c):
        i = (turn - z // 2) % 4
        return (yl, 3 * c + i, x, yh, z % 2) if i < 3 else None

    return target


def from_column(turn):
    def target(yl, z, x, yh, c):
        if z >= 6:
            return None
        r = (turn - z % 3) % 4
        return (yl, 2 * r + c, x, yh, z // 3)

    return target


def to_width(step):
    def target(yl, z, x, yh, c):
        width = 4 * c + x + step
        if z >= 6 or not 0 <= width < 8:
            return None
        return (yl, z, width % 4, yh, width // 4)

    return target


def across(yl, z, x, yh, c):
    return (1 - yl, z, x, yh, c) if z < 6 else None


def dot_nt(a, b):
    return lax.dot_general(a, b, (((1,), (1,)), ((), ())), preferred_element_type=jnp.float32)


def fold_lanes(op, block):
    out = block[:, :HEAD]
    for start in range(HEAD, block.shape[1], HEAD):
        out = op(out, block[:, start : start + HEAD])
    return out


def weights_of(scores, peak):
    parts = []
    for start in range(0, scores.shape[1], HEAD):
        parts.append(jnp.exp2((scores[:, start : start + HEAD] - peak) * RATE))
    return functools.reduce(jnp.add, parts), jnp.concatenate(parts, axis=1).astype(jnp.bfloat16)


def column_kernel(turns, params, lists, *refs):
    many = len(turns)
    queries, blocks, words = refs[:many], refs[many : many + 15], refs[many + 15]
    outs = refs[many + 16 : 2 * many + 16]
    pool, scores, sems = refs[2 * many + 16 :]
    copies, start = [], 0
    for n, block in enumerate(blocks):
        place = pl.ds(start, block.shape[0])
        copies.append(pltpu.make_async_copy(block, pool.at[place], sems.at[n]))
        start += block.shape[0]
    for copy in copies:
        copy.start()
    yl, width, head, text_len = params[0], params[1], params[2], params[3]
    for copy in copies:
        copy.wait()
    row = lax.broadcasted_iota(jnp.int32, (TILE, 256), 1)
    live = text_token(row) < text_len

    def key_row(entry):
        height = (entry >> 4) - yl * 4
        slot = jnp.where((height >= 0) & (height < 4), (height + head) & 3, 4)
        shift = ((entry >> 1) & 7) - width
        slot = slot + jnp.where(shift == 0, 0, jnp.where(shift < 0, 5, 10))
        return jnp.clip(slot, 0, 14) * BLOCK + (entry & 1) * TILE

    for spot, turn in enumerate(turns):
        found = []
        for half in range(2):
            base = (turn * 2 + half) * SLOTS
            rows, valid = [], []
            for j in range(SLOTS):
                entry = lists[base + j]
                valid.append(entry >= 0)
                rows.append(key_row(jnp.where(entry >= 0, entry, lists[base])))
            found.append((rows, valid))
        peaks = []
        for half, (rows, valid) in enumerate(found):
            q = queries[spot][half * TILE : (half + 1) * TILE, :]
            s = jnp.where(live, dot_nt(q, words[0]), -jnp.inf)
            scores[half, SLOTS, :, :256] = s
            peak = fold_lanes(jnp.maximum, s)
            for j in range(SLOTS):
                s = dot_nt(q, pool[pl.ds(pl.multiple_of(rows[j], 16), TILE), :])
                scores[half, j] = s
                s = fold_lanes(jnp.maximum, s)
                peak = jnp.maximum(peak, jnp.where(valid[j], s, -jnp.inf))
            peaks.append(jnp.max(peak, axis=1, keepdims=True))
        for half, (rows, valid) in enumerate(found):
            peak = jnp.broadcast_to(peaks[half], (TILE, HEAD))
            total, w = weights_of(scores[half, SLOTS, :, :256], peak)
            summed = jnp.dot(w, words[1], preferred_element_type=jnp.float32)
            for j in range(SLOTS):
                more, w = weights_of(scores[half, j], jnp.where(valid[j], peak, jnp.inf))
                total = total + more
                v = pool[pl.ds(pl.multiple_of(rows[j] + ROWS, 16), TILE), :]
                summed = summed + jnp.dot(w, v, preferred_element_type=jnp.float32)
            total = jnp.sum(total, axis=1, keepdims=True)
            outs[spot][half * TILE : (half + 1) * TILE, :] = (summed / total).astype(jnp.bfloat16)
        outs[spot][ROWS:, :] = jnp.zeros((PIECE - ROWS, HEAD), jnp.bfloat16)


def attend_column(turns, params, lists, queries, blocks, words):
    smem = pl.BlockSpec(memory_space=pltpu.SMEM)
    vmem = pl.BlockSpec(memory_space=pltpu.VMEM)
    hbm = pl.BlockSpec(memory_space=pl.ANY)
    count = len(turns)
    return pl.pallas_call(
        functools.partial(column_kernel, turns),
        out_shape=[jax.ShapeDtypeStruct((PIECE, HEAD), jnp.bfloat16)] * count,
        in_specs=[smem, smem] + [vmem] * count + [hbm] * 15 + [vmem],
        out_specs=[vmem] * count,
        scratch_shapes=[
            pltpu.VMEM((15 * BLOCK, HEAD), jnp.bfloat16),
            pltpu.VMEM((2, SLOTS + 1, TILE, TILE), jnp.float32),
            pltpu.SemaphoreType.DMA((15,)),
        ],
        compiler_params=pltpu.CompilerParams(vmem_limit_bytes=VMEM),
        cost_estimate=COST,
        name="attend_column",
    )(params, lists, *queries, *blocks, words)


def text_token(row):
    yl, x, z = row >> 7, (row >> 5) & 3, ((row >> 2) & 3) * 2 + ((row >> 4) & 1)
    return ((yl * 8 + z) * 4 + x) * 4 + (row & 3)


def stats_of(peak, total):
    lane = lax.broadcasted_iota(jnp.int32, (peak.shape[0], HEAD), 1)
    return jnp.where(lane == 0, peak, jnp.where(lane == 1, total, 0.0))


def text_kernel(limit, words, *refs):
    blocks, out = refs[:4], refs[4]
    row = lax.broadcasted_iota(jnp.int32, (256, 256), 1)
    q = words[0]
    scores = [dot_nt(q, block[:ROWS, :]) for block in blocks]
    scores.append(jnp.where(text_token(row) < limit[0], dot_nt(q, words[1]), -jnp.inf))
    values = [block[ROWS : 2 * ROWS, :] for block in blocks] + [words[2]]
    peak = functools.reduce(jnp.maximum, [fold_lanes(jnp.maximum, s) for s in scores])
    peak = jnp.max(peak, axis=1, keepdims=True)
    total, summed = 0.0, 0.0
    for s, v in zip(scores, values):
        more, w = weights_of(s, peak)
        total = total + more
        summed = summed + jnp.dot(w, v, preferred_element_type=jnp.float32)
    stats = stats_of(peak, jnp.sum(total, axis=1, keepdims=True))
    out[:, :HEAD] = summed
    out[:, HEAD:] = stats


def attend_text(limit, words, blocks):
    vmem = pl.BlockSpec(memory_space=pltpu.VMEM)
    return pl.pallas_call(
        text_kernel,
        out_shape=jax.ShapeDtypeStruct((256, 256), jnp.float32),
        in_specs=[pl.BlockSpec(memory_space=pltpu.SMEM)] + [vmem] * 5,
        out_specs=vmem,
        compiler_params=pltpu.CompilerParams(vmem_limit_bytes=VMEM),
        cost_estimate=COST,
        name="attend_text",
    )(limit, words, *blocks)


def merge_kernel(parts, out):
    peak = functools.reduce(jnp.maximum, [parts[n, :, 128:129] for n in range(16)])
    total, summed = 0.0, 0.0
    for n in range(16):
        scale = jnp.exp2((parts[n, :, 128:129] - peak) * RATE)
        total = total + parts[n, :, 129:130] * scale
        summed = summed + parts[n, :, :HEAD] * scale
    out[...] = (summed / total).astype(jnp.bfloat16)


def merge_text(parts):
    vmem = pl.BlockSpec(memory_space=pltpu.VMEM)
    return pl.pallas_call(
        merge_kernel,
        out_shape=jax.ShapeDtypeStruct((16, HEAD), jnp.bfloat16),
        in_specs=[vmem],
        out_specs=vmem,
        name="merge_text",
    )(parts)


def after(value, *others):
    return lax.optimization_barrier((value, *others))[0]


def shards(q_video, k_video, v_video, q_text, k_text, v_text, tile_lists, text_len):
    yl, z, x, c = (lax.axis_index(name) for name in ("yl", "z", "x", "c"))
    r, head = z // 2, z % 3

    def head_of(array, turn):
        i = jnp.minimum((turn - r) % 4, 2)
        return lax.dynamic_slice(array, (0, i * HEAD), (array.shape[0], HEAD))

    text = jnp.concatenate([q_text, k_text, v_text, jnp.zeros_like(q_text)], axis=0)
    listed = jnp.pad(tile_lists.astype(jnp.bfloat16).reshape(1, 16), ((0, 15), (0, 112)))
    own, queries, left, right = {}, {}, {}, {}
    for turn, behind in ((0, None), (2, None), (1, 0), (3, 2)):
        block = [head_of(array, turn) for array in (k_video, v_video, text)]
        block = jnp.concatenate(block, axis=0)
        if behind is not None:
            block = after(block, own[behind])
        own[turn] = send(block, to_column(turn))
    own[4] = send(
        lax.select_n((jnp.where(yl == 0, 3, 0) + head) % 4, *(own[turn] for turn in range(4))),
        across,
    )
    for turn, behind in ((0, None), (2, None), (1, 0), (3, 2), (4, 1)):
        block = own[turn] if behind is None else after(own[turn], left[behind], right[behind])
        left[turn] = send(block, to_width(1))
        right[turn] = send(block, to_width(-1))
    for turn, behind in ((0, own[1]), (2, own[3]), (1, left[2]), (3, left[1])):
        piece = jnp.concatenate([head_of(q_video, turn), listed], axis=0)
        queries[turn] = send(after(piece, behind), to_column(turn))
    own, left, right = ([group[n] for n in range(5)] for group in (own, left, right))
    blocks = own + left + right

    held = jnp.stack([block[2 * ROWS :] for block in own[:4]])
    held = lax.dynamic_slice(jnp.concatenate([held, held]), (head, 0, 0), (4, 12, HEAD))
    held = held.reshape(4, 3, 4, HEAD).transpose(1, 0, 2, 3).reshape(3, 16, HEAD)
    held = after(held, left[0], right[0], left[2], right[2])
    held = lax.all_to_all(jnp.broadcast_to(held, (16, 3, 16, HEAD)), GROUP, 0, 0, tiled=True)
    held = held.transpose(1, 0, 2, 3).reshape(3, 256, HEAD)

    first_column = (yl == 0) & (x == 0) & (c == 0)
    limit = jnp.where(first_column, text_len[0], 0).astype(jnp.int32)[None]
    held = after(held, left[1], right[1], left[3], right[3], queries[0], queries[2])
    packed = after(attend_text(limit, held, own[:4]), left[4], right[4], queries[1], queries[3])
    packed = lax.all_to_all(packed.reshape(16, 16, 256), GROUP, 0, 0, tiled=True)
    text_done = merge_text(packed)

    lists = jnp.stack([queries[turn][ROWS, :16] for turn in range(4)]).astype(jnp.int32).reshape(64)
    params = jnp.stack([yl, 4 * c + x, head, text_len[0]]).astype(jnp.int32)
    back = []
    for turns in CALLS:
        some = [queries[turn] for turn in turns]
        if back:
            some[0] = after(some[0], *(back[:2] if len(back) > 2 else [text_done]))
        done = attend_column(turns, params, lists, some, blocks, held[1:])
        for turn, piece in zip(turns, done):
            mine = lax.dynamic_slice(text_done, ((turn - head) % 4 * 4, 0), (4, HEAD))
            piece = lax.dynamic_update_slice(piece, jnp.pad(mine, ((0, 12), (0, 0))), (ROWS, 0))
            back.append(send(piece, from_column(turn)))
    heads = [lax.select_n((r + i) % 4, *back) for i in range(3)]
    out = jnp.concatenate(heads, axis=1)
    video_out = lax.all_to_all(out[:ROWS], ("yh", "c"), split_axis=0, concat_axis=1, tiled=True)
    return (video_out, out[ROWS : ROWS + 4])


def solution(mesh):
    fine = Mesh(mesh.devices.reshape(SIZES), NAMES)
    tile, head = ("yl", "z", "x"), ("yh", "c")
    split = P(tile, head)
    in_specs = (split,) * 6 + (P(tile, None), P())
    out_specs = (P(tile + head, None), split)
    return jax.shard_map(shards, mesh=fine, in_specs=in_specs, out_specs=out_specs, check_vma=False)
```

time: 977 us -> 209 us (0.21)
  the two profiles are of different devices: /device:TPU:8 before, /device:TPU:2 now
where the time goes in v1:
time: 209 us; the launch traced here: 208 us
  starting transfers between devices  108 us (52%)
  waiting for transfers between devices  39.4 us (19%)
  Pallas kernels  32.9 us (16%)
  local copies, waits for them, and re-layouts  19.8 us (9%)
  other arithmetic  5.3 us (3%)
    ppermute x23, starting transfers between devices, send(): return lax.ppermute(value, NAMES, pairs_of(target))  86 us
    pallas_call x3, Pallas kernels, attend_column(): pl.pallas_call(functools.partial(column_kernel, turns), out_shape=[jax.Sh...  29.4 us
    ppermute x23, waiting for transfers between devices, send(): return lax.ppermute(value, NAMES, pairs_of(target))  20.1 us
    all_to_all x1, waiting for transfers between devices, shards(): lax.all_to_all(out[:ROWS], ('yh', 'c'), split_axis=0, concat_axis=1, tile...  19.2 us
    unnamed x39, local copies, waits for them, and re-layouts  8.54 us
    all_to_all x1, starting transfers between devices, shards(): lax.all_to_all(packed.reshape(16, 16, 256), GROUP, 0, 0, tiled=True)  8.21 us
    all_to_all x1, starting transfers between devices, shards(): lax.all_to_all(jnp.broadcast_to(held, (16, 3, 16, HEAD)), GROUP, 0, 0, ti...  7.68 us
    all_to_all x1, starting transfers between devices, shards(): lax.all_to_all(out[:ROWS], ('yh', 'c'), split_axis=0, concat_axis=1, tile...  6.24 us
  transfers between devices with their start and end apart: 26, of which 6 were waited for; matrix products, arithmetic and copies ran while one was open for 5% of the time, Pallas kernels for 15%

profile of v1, /device:TPU:2, one launch (start us, length us, event | category | flops | bytes accessed | tf_op | source)
XLA Modules:
  0.0 207.6 jit_solution(17680454343780402194)
XLA Ops:
  0.8 0.8 maximum_maximum_fusion
  1.6 1.6 constant_dynamic-slice_fusion.11
  3.2 0.7 collective-permute-start
  4.0 6.7 %collective-permute-start.3 = (bf16[1552,128]{1,0:T(8,128)(2,1)S(1)}, bf16[1552,128]{1,0:T(8,128)(2,1)S(1)}, u32[]{:S(2)}, u32[]{:S(2)}) collective-permute-start(bf16[1552,128]{1,0:T(8,128)(2,1)S(1)} %pad_maximum_fusion.3), channel_id=1, source_target_pairs={{0,64},{1,160},{2,66},{3,162},{4,68},{5,164},{6,70},{7,166},{8,72}... | collective-permute-start | bytes 1191944 | tf_op jit(solution)/shard_map/ppermute | solution.py:41
  10.7 0.8 pad_maximum_fusion.1
  11.5 0.8 pad_maximum_fusion.4
  12.2 19.1 %collective-permute-start.1 = (bf16[1552,128]{1,0:T(8,128)(2,1)}, bf16[1552,128]{1,0:T(8,128)(2,1)S(1)}, u32[]{:S(2)}, u32[]{:S(2)}) collective-permute-start(bf16[1552,128]{1,0:T(8,128)(2,1)} %pad_maximum_fusion.1), channel_id=1, source_target_pairs={{0,32},{1,128},{2,34},{3,130},{4,36},{5,132},{6,38},{7,134},{8,40}... | collective-permute-start | bytes 1191944 | tf_op jit(solution)/shard_map/ppermute | solution.py:41
  31.4 1.3 collective-permute-start.6
  32.7 2.4 %collective-permute-start.9 = (bf16[1552,128]{1,0:T(8,128)(2,1)S(1)}, bf16[1552,128]{1,0:T(8,128)(2,1)S(1)}, u32[]{:S(2)}, u32[]{:S(2)}) collective-permute-start(bf16[1552,128]{1,0:T(8,128)(2,1)S(1)} %collective-permute-done.refs_2_.refs_0_.refs_1_), channel_id=1, source_target_pairs={{1,24},{3,26},{5,28},{7,30},{8,0},{9,1},{10,2},{11,3},{12,4},{13,5... | collective-permute-start | bytes 1191944 | tf_op jit(solution)/shard_map/ppermute | solution.py:41
  35.1 3.4 %collective-permute-start.8 = (bf16[1552,128]{1,0:T(8,128)(2,1)S(1)}, bf16[1552,128]{1,0:T(8,128)(2,1)S(1)}, u32[]{:S(2)}, u32[]{:S(2)}) collective-permute-start(bf16[1552,128]{1,0:T(8,128)(2,1)S(1)} %collective-permute-done.refs_2_.refs_0_.refs_1_), channel_id=1, source_target_pairs={{0,8},{1,9},{2,10},{3,11},{4,12},{5,13},{6,14},{7,15},{8,16},{9,17... | collective-permute-start | bytes 1191944 | tf_op jit(solution)/shard_map/ppermute | solution.py:41
  38.9 0.8 fusion.3
  39.7 2.5 %collective-permute-start.13 = (bf16[1552,128]{1,0:T(8,128)(2,1)S(1)}, bf16[1552,128]{1,0:T(8,128)(2,1)S(1)}, u32[]{:S(2)}, u32[]{:S(2)}) collective-permute-start(bf16[1552,128]{1,0:T(8,128)(2,1)S(1)} %collective-permute-done.3.refs_4_.refs_2_.refs_3_), channel_id=1, source_target_pairs={{1,24},{3,26},{5,28},{7,30},{8,0},{9,1},{10,2},{11,3},{12,4},{13,5... | collective-permute-start | bytes 1191944 | tf_op jit(solution)/shard_map/ppermute | solution.py:41
  42.2 4.4 %collective-permute-done.1.refs_3_.refs_1_.refs_2_ = bf16[1552,128]{1,0:T(8,128)(2,1)S(1)} collective-permute-done((bf16[1552,128]{1,0:T(8,128)(2,1)}, bf16[1552,128]{1,0:T(8,128)(2,1)S(1)}, u32[]{:S(2)}, u32[]{:S(2)}) %collective-permute-start.1) | collective-permute-done | bytes 397344 | tf_op jit(solution)/shard_map/ppermute | solution.py:41
  46.5 3.4 %collective-permute-start.4 = (bf16[1552,128]{1,0:T(8,128)(2,1)S(1)}, bf16[1552,128]{1,0:T(8,128)(2,1)S(1)}, u32[]{:S(2)}, u32[]{:S(2)}) collective-permute-start(bf16[1552,128]{1,0:T(8,128)(2,1)S(1)} %collective-permute-done.3.refs_4_.refs_2_.refs_3_), channel_id=1, source_target_pairs={{0,8},{1,9},{2,10},{3,11},{4,12},{5,13},{6,14},{7,15},{8,16},{9,17... | collective-permute-start | bytes 1191944 | tf_op jit(solution)/shard_map/ppermute | solution.py:41
  50.0 2.5 %collective-permute-start.15 = (bf16[1552,128]{1,0:T(8,128)(2,1)S(1)}, bf16[1552,128]{1,0:T(8,128)(2,1)S(1)}, u32[]{:S(2)}, u32[]{:S(2)}) collective-permute-start(bf16[1552,128]{1,0:T(8,128)(2,1)S(1)} %collective-permute-done.1.refs_3_.refs_1_.refs_2_), channel_id=1, source_target_pairs={{1,24},{3,26},{5,28},{7,30},{8,0},{9,1},{10,2},{11,3},{12,4},{13,5... | collective-permute-start | bytes 1191944 | tf_op jit(solution)/shard_map/ppermute | solution.py:41
  52.4 5.9 %collective-permute-start.10 = (bf16[1552,128]{1,0:T(8,128)(2,1)S(1)}, bf16[1552,128]{1,0:T(8,128)(2,1)S(1)}, u32[]{:S(2)}, u32[]{:S(2)}) collective-permute-start(bf16[1552,128]{1,0:T(8,128)(2,1)S(1)} %collective-permute-done.1.refs_3_.refs_1_.refs_2_), channel_id=1, source_target_pairs={{0,8},{1,9},{2,10},{3,11},{4,12},{5,13},{6,14},{7,15},{8,16},{9,17... | collective-permute-start | bytes 1191944 | tf_op jit(solution)/shard_map/ppermute | solution.py:41
  58.3 1.3 collective-permute-start.2
  59.8 3.5 %collective-permute-start.12 = (bf16[1552,128]{1,0:T(8,128)(2,1)S(1)}, bf16[1552,128]{1,0:T(8,128)(2,1)}, u32[]{:S(2)}, u32[]{:S(2)}) collective-permute-start(bf16[1552,128]{1,0:T(8,128)(2,1)S(1)} %select_select_fusion), channel_id=1, source_target_pairs={{0,256},{1,257},{2,258},{3,259},{4,260},{5,261},{6,262},{7,263},{8... | collective-permute-start | bytes 1191944 | tf_op jit(solution)/shard_map/ppermute | solution.py:41
  63.3 1.9 collective-permute-start.17
  65.3 0.7 copy-done
  66.0 6.4 %collective-permute-start.14 = (bf16[1552,128]{1,0:T(8,128)(2,1)S(1)}, bf16[1552,128]{1,0:T(8,128)(2,1)}, u32[]{:S(2)}, u32[]{:S(2)}) collective-permute-start(bf16[1552,128]{1,0:T(8,128)(2,1)S(1)} %collective-permute-done.6.refs_5_.refs_3_.refs_4_), channel_id=1, source_target_pairs={{0,8},{1,9},{2,10},{3,11},{4,12},{5,13},{6,14},{7,15},{8,16},{9,17... | collective-permute-start | bytes 1191944 | tf_op jit(solution)/shard_map/ppermute | solution.py:41
  72.4 0.7 copy-done.4
  73.2 1.9 collective-permute-start.7
  75.1 1.9 collective-permute-start.18
  77.1 3.9 %collective-permute-start.16 = (bf16[1552,128]{1,0:T(8,128)(2,1)}, bf16[1552,128]{1,0:T(8,128)(2,1)}, u32[]{:S(2)}, u32[]{:S(2)}) collective-permute-start(bf16[1552,128]{1,0:T(8,128)(2,1)} %collective-permute-done.12.refs_6_.refs_5_), channel_id=1, source_target_pairs={{0,8},{1,9},{2,10},{3,11},{4,12},{5,13},{6,14},{7,15},{8,16},{9,17... | collective-permute-start | bytes 1191944 | tf_op jit(solution)/shard_map/ppermute | solution.py:41
  81.0 0.7 broadcast_in_dim.10
  81.7 7.7 %all-to-all-start = ((bf16[16,3,16,128]{3,2,1,0:T(8,128)(2,1)}), bf16[16,3,16,128]{3,2,1,0:T(8,128)(2,1)}, u32[]{:S(2)}, u32[]{:S(2)}) async-start(bf16[16,3,16,128]{3,2,1,0:T(8,128)(2,1)} %broadcast_in_dim.10), calls=%async_computation | async-start | bytes 393216 | tf_op jit(solution)/shard_map/all_to_all | solution.py:278
  89.4 3.0 %collective-permute-start.5 = (bf16[784,128]{1,0:T(8,128)(2,1)}, bf16[784,128]{1,0:T(8,128)(2,1)}, u32[]{:S(2)}, u32[]{:S(2)}) collective-permute-start(bf16[784,128]{1,0:T(8,128)(2,1)} %get-tuple-element.20), channel_id=1, source_target_pairs={{0,32},{1,128},{2,34},{3,130},{4,36},{5,132},{6,38},{7,134},{8,40}... | collective-permute-start | bytes 602120 | tf_op jit(solution)/shard_map/ppermute | solution.py:41
  92.5 1.3 collective-permute-start.11
  94.5 0.9 copy.18
  95.5 1.7 attend_text.1
  97.2 0.7 copy-done.7
  97.9 5.8 %collective-permute-done.5.refs_1_ = bf16[784,128]{1,0:T(8,128)(2,1)} collective-permute-done((bf16[784,128]{1,0:T(8,128)(2,1)}, bf16[784,128]{1,0:T(8,128)(2,1)}, u32[]{:S(2)}, u32[]{:S(2)}) %collective-permute-start.5) | collective-permute-done | bytes 200736 | tf_op jit(solution)/shard_map/ppermute | solution.py:41
  103.7 1.6 collective-permute-done.11.refs_0_
  105.3 8.2 %all-to-all-start.1 = ((f32[16,16,256]{2,1,0:T(8,128)}), f32[16,16,256]{2,1,0:T(8,128)}, u32[]{:S(2)}, u32[]{:S(2)}) async-start(f32[16,16,256]{2,1,0:T(8,128)} %bitcast.43), calls=%async_computation.1 | async-start | bytes 524288 | tf_op jit(solution)/shard_map/all_to_all | solution.py:285
  113.5 0.7 slice.46
  114.2 0.7 slice.48
  114.9 0.7 slice.47
  115.6 0.7 slice.49
  116.4 1.0 copy-done.1
  117.4 1.0 copy-done.5
  118.4 11.9 %attend_column.3 = (bf16[784,128]{1,0:T(8,128)(2,1)S(1)}, bf16[784,128]{1,0:T(8,128)(2,1)S(1)}) custom-call(s32[4]{0:T(128)S(1)} %pad_add_fusion.params, s32[64]{0:T(128)S(1)} %reshape.31.lists, bf16[784,128]{1,0:T(8,128)(2,1)} %collective-permute-done.2.refs_0_, bf16[784,128]{1,0:T(8,128)(2,1)} %collective-permute-done.5.refs_1_, ...), custom_call_target="tpu_custom_call" | custom-call | flops 1048576 | bytes 65536 | tf_op jit(solution)/shard_map/attend_column/pallas_call | solution.py:160
  130.3 0.7 copy-done.10
  131.0 0.7 copy-done.11
  131.7 1.7 merge_text.1
  133.4 0.8 constant_dynamic-slice_fusion
  134.2 0.6 constant_dynamic-update-slice_fusion.10
  134.8 2.2 %collective-permute-start.20 = (bf16[784,128]{1,0:T(8,128)(2,1)}, bf16[784,128]{1,0:T(8,128)(2,1)S(1)}, u32[]{:S(2)}, u32[]{:S(2)}) collective-permute-start(bf16[784,128]{1,0:T(8,128)(2,1)} %constant_dynamic-update-slice_fusion.10), channel_id=1, source_target_pairs={{0,64},{1,96},{2,66},{3,98},{4,68},{5,100},{6,70},{7,102},{8,72},{... | collective-permute-start | bytes 602120 | tf_op jit(solution)/shard_map/ppermute | solution.py:41
  136.9 0.6 constant_dynamic-update-slice_fusion.11
  137.5 1.6 collective-permute-start.19
  139.1 1.0 copy-done.2
  140.1 1.0 copy-done.6
  141.1 0.9 copy-done.9
  142.0 8.5 %attend_column.4 = bf16[784,128]{1,0:T(8,128)(2,1)} custom-call(s32[4]{0:T(128)S(1)} %pad_add_fusion.params, s32[64]{0:T(128)S(1)} %reshape.31.lists, bf16[784,128]{1,0:T(8,128)(2,1)S(1)} %copy-done.9, bf16[1552,128]{1,0:T(8,128)(2,1)S(1)} %collective-permute-done.refs_2_.refs_0_.refs_1_, ...), custom_call_target="tpu_custom_call" | custom-call | flops 1048576 | bytes 65536 | tf_op jit(solution)/shard_map/attend_column/pallas_call | solution.py:160
  150.5 0.6 constant_dynamic-update-slice_fusion.9
  151.1 7.9 %collective-permute-start.21 = (bf16[784,128]{1,0:T(8,128)(2,1)}, bf16[784,128]{1,0:T(8,128)(2,1)}, u32[]{:S(2)}, u32[]{:S(2)}) collective-permute-start(bf16[784,128]{1,0:T(8,128)(2,1)} %constant_dynamic-update-slice_fusion.9), channel_id=1, source_target_pairs={{0,128},{1,160},{2,130},{3,162},{4,132},{5,164},{6,134},{7,166},{8... | collective-permute-start | bytes 602120 | tf_op jit(solution)/shard_map/ppermute | solution.py:41
  159.1 9.0 %attend_column.5 = bf16[784,128]{1,0:T(8,128)(2,1)} custom-call(s32[4]{0:T(128)S(1)} %pad_add_fusion.params, s32[64]{0:T(128)S(1)} %reshape.31.lists, bf16[784,128]{1,0:T(8,128)(2,1)} %collective-permute-done.11.refs_0_, bf16[1552,128]{1,0:T(8,128)(2,1)S(1)} %collective-permute-done.refs_2_.refs_0_.refs_1_, ...), custom_call_target="tpu_custom_call" | custom-call | flops 1048576 | bytes 65536 | tf_op jit(solution)/shard_map/attend_column/pallas_call | solution.py:160
  168.7 1.3 collective-permute-start.22
  170.1 8.4 %collective-permute-done.22 = bf16[784,128]{1,0:T(8,128)(2,1)S(1)} collective-permute-done((bf16[784,128]{1,0:T(8,128)(2,1)}, bf16[784,128]{1,0:T(8,128)(2,1)S(1)}, u32[]{:S(2)}, u32[]{:S(2)}) %collective-permute-start.22) | collective-permute-done | bytes 200736 | tf_op jit(solution)/shard_map/ppermute | solution.py:41
  178.5 1.2 select_select_fusion.3
  179.8 0.9 slice.54
  180.6 6.2 %all-to-all-start.2 = ((bf16[8,96,384]{2,1,0:T(8,128)(2,1)}), bf16[8,96,384]{2,1,0:T(8,128)(2,1)S(1)}, u32[]{:S(2)}, u32[]{:S(2)}) async-start(bf16[8,96,384]{2,1,0:T(8,128)(2,1)} %bitcast.15), calls=%async_computation.2 | async-start | bytes 1179648 | tf_op jit(solution)/shard_map/all_to_all | solution.py:302
  187.5 19.2 %all-to-all-done.2 = bf16[8,96,384]{2,1,0:T(8,128)(2,1)S(1)} async-done(((bf16[8,96,384]{2,1,0:T(8,128)(2,1)}), bf16[8,96,384]{2,1,0:T(8,128)(2,1)S(1)}, u32[]{:S(2)}, u32[]{:S(2)}) %all-to-all-start.2) | async-done | bytes 589856 | tf_op jit(solution)/shard_map/all_to_all | solution.py:302
  206.7 0.9 copy.20
  (70 shorter events, 2.2 us)
Async XLA Ops:
  3.2 9.0 %collective-permute-start = (bf16[1552,128]{1,0:T(8,128)(2,1)S(1)}, bf16[1552,128]{1,0:T(8,128)(2,1)S(1)}, u32[]{:S(2)}, u32[]{:S(2)}) collective-permute-start(bf16[1552,128]{1,0:T(8,128)(2,1)S(1)} %pad_maximum_fusion.2), channel_id=1, source_target_pairs={{0,0},{1,96},{2,2},{3,98},{4,4},{5,100},{6,6},{7,102},{8,8},{9,104... | collective-permute-start | bytes 1191944 | tf_op jit(solution)/shard_map/ppermute | solution.py:41
  4.0 27.4 %collective-permute-start.3 = (bf16[1552,128]{1,0:T(8,128)(2,1)S(1)}, bf16[1552,128]{1,0:T(8,128)(2,1)S(1)}, u32[]{:S(2)}, u32[]{:S(2)}) collective-permute-start(bf16[1552,128]{1,0:T(8,128)(2,1)S(1)} %pad_maximum_fusion.3), channel_id=1, source_target_pairs={{0,64},{1,160},{2,66},{3,162},{4,68},{5,164},{6,70},{7,166},{8,72}... | collective-permute-start | bytes 1191944 | tf_op jit(solution)/shard_map/ppermute | solution.py:41
  10.7 27.9 %copy-start.12 = (bf16[768,384]{1,0:T(8,128)(2,1)S(1)}, bf16[768,384]{1,0:T(8,128)(2,1)}, u32[]{:S(2)}) copy-start(bf16[768,384]{1,0:T(8,128)(2,1)} %param.8) | copy-start | bytes 1769476
  12.2 26.5 %copy-start.15 = (s32[2,8]{1,0:T(2,128)S(1)}, s32[2,8]{1,0:T(2,128)}, u32[]{:S(2)}) copy-start(s32[2,8]{1,0:T(2,128)} %param.14) | copy-start | bytes 196
  12.2 34.3 %collective-permute-start.1 = (bf16[1552,128]{1,0:T(8,128)(2,1)}, bf16[1552,128]{1,0:T(8,128)(2,1)S(1)}, u32[]{:S(2)}, u32[]{:S(2)}) collective-permute-start(bf16[1552,128]{1,0:T(8,128)(2,1)} %pad_maximum_fusion.1), channel_id=1, source_target_pairs={{0,32},{1,128},{2,34},{3,130},{4,36},{5,132},{6,38},{7,134},{8,40}... | collective-permute-start | bytes 1191944 | tf_op jit(solution)/shard_map/ppermute | solution.py:41
  31.4 26.9 %collective-permute-start.6 = (bf16[1552,128]{1,0:T(8,128)(2,1)}, bf16[1552,128]{1,0:T(8,128)(2,1)S(1)}, u32[]{:S(2)}, u32[]{:S(2)}) collective-permute-start(bf16[1552,128]{1,0:T(8,128)(2,1)} %pad_maximum_fusion.4), channel_id=1, source_target_pairs={{64,64},{65,160},{66,66},{67,162},{68,68},{69,164},{70,70},{71,166... | collective-permute-start | bytes 1191944 | tf_op jit(solution)/shard_map/ppermute | solution.py:41
  32.7 17.3 %collective-permute-start.9 = (bf16[1552,128]{1,0:T(8,128)(2,1)S(1)}, bf16[1552,128]{1,0:T(8,128)(2,1)S(1)}, u32[]{:S(2)}, u32[]{:S(2)}) collective-permute-start(bf16[1552,128]{1,0:T(8,128)(2,1)S(1)} %collective-permute-done.refs_2_.refs_0_.refs_1_), channel_id=1, source_target_pairs={{1,24},{3,26},{5,28},{7,30},{8,0},{9,1},{10,2},{11,3},{12,4},{13,5... | collective-permute-start | bytes 1191944 | tf_op jit(solution)/shard_map/ppermute | solution.py:41
  35.1 14.8 %collective-permute-start.8 = (bf16[1552,128]{1,0:T(8,128)(2,1)S(1)}, bf16[1552,128]{1,0:T(8,128)(2,1)S(1)}, u32[]{:S(2)}, u32[]{:S(2)}) collective-permute-start(bf16[1552,128]{1,0:T(8,128)(2,1)S(1)} %collective-permute-done.refs_2_.refs_0_.refs_1_), channel_id=1, source_target_pairs={{0,8},{1,9},{2,10},{3,11},{4,12},{5,13},{6,14},{7,15},{8,16},{9,17... | collective-permute-start | bytes 1191944 | tf_op jit(solution)/shard_map/ppermute | solution.py:41
  39.7 20.0 %collective-permute-start.13 = (bf16[1552,128]{1,0:T(8,128)(2,1)S(1)}, bf16[1552,128]{1,0:T(8,128)(2,1)S(1)}, u32[]{:S(2)}, u32[]{:S(2)}) collective-permute-start(bf16[1552,128]{1,0:T(8,128)(2,1)S(1)} %collective-permute-done.3.refs_4_.refs_2_.refs_3_), channel_id=1, source_target_pairs={{1,24},{3,26},{5,28},{7,30},{8,0},{9,1},{10,2},{11,3},{12,4},{13,5... | collective-permute-start | bytes 1191944 | tf_op jit(solution)/shard_map/ppermute | solution.py:41
  46.5 16.7 %collective-permute-start.4 = (bf16[1552,128]{1,0:T(8,128)(2,1)S(1)}, bf16[1552,128]{1,0:T(8,128)(2,1)S(1)}, u32[]{:S(2)}, u32[]{:S(2)}) collective-permute-start(bf16[1552,128]{1,0:T(8,128)(2,1)S(1)} %collective-permute-done.3.refs_4_.refs_2_.refs_3_), channel_id=1, source_target_pairs={{0,8},{1,9},{2,10},{3,11},{4,12},{5,13},{6,14},{7,15},{8,16},{9,17... | collective-permute-start | bytes 1191944 | tf_op jit(solution)/shard_map/ppermute | solution.py:41
  50.0 15.3 %collective-permute-start.15 = (bf16[1552,128]{1,0:T(8,128)(2,1)S(1)}, bf16[1552,128]{1,0:T(8,128)(2,1)S(1)}, u32[]{:S(2)}, u32[]{:S(2)}) collective-permute-start(bf16[1552,128]{1,0:T(8,128)(2,1)S(1)} %collective-permute-done.1.refs_3_.refs_1_.refs_2_), channel_id=1, source_target_pairs={{1,24},{3,26},{5,28},{7,30},{8,0},{9,1},{10,2},{11,3},{12,4},{13,5... | collective-permute-start | bytes 1191944 | tf_op jit(solution)/shard_map/ppermute | solution.py:41
  52.4 20.0 %collective-permute-start.10 = (bf16[1552,128]{1,0:T(8,128)(2,1)S(1)}, bf16[1552,128]{1,0:T(8,128)(2,1)S(1)}, u32[]{:S(2)}, u32[]{:S(2)}) collective-permute-start(bf16[1552,128]{1,0:T(8,128)(2,1)S(1)} %collective-permute-done.1.refs_3_.refs_1_.refs_2_), channel_id=1, source_target_pairs={{0,8},{1,9},{2,10},{3,11},{4,12},{5,13},{6,14},{7,15},{8,16},{9,17... | collective-permute-start | bytes 1191944 | tf_op jit(solution)/shard_map/ppermute | solution.py:41
  58.3 18.7 %collective-permute-start.2 = (bf16[784,128]{1,0:T(8,128)(2,1)S(1)}, bf16[784,128]{1,0:T(8,128)(2,1)}, u32[]{:S(2)}, u32[]{:S(2)}) collective-permute-start(bf16[784,128]{1,0:T(8,128)(2,1)S(1)} %get-tuple-element.19), channel_id=1, source_target_pairs={{0,0},{1,96},{2,2},{3,98},{4,4},{5,100},{6,6},{7,102},{8,8},{9,104... | collective-permute-start | bytes 602120 | tf_op jit(solution)/shard_map/ppermute | solution.py:41
  59.8 15.3 %collective-permute-start.12 = (bf16[1552,128]{1,0:T(8,128)(2,1)S(1)}, bf16[1552,128]{1,0:T(8,128)(2,1)}, u32[]{:S(2)}, u32[]{:S(2)}) collective-permute-start(bf16[1552,128]{1,0:T(8,128)(2,1)S(1)} %select_select_fusion), channel_id=1, source_target_pairs={{0,256},{1,257},{2,258},{3,259},{4,260},{5,261},{6,262},{7,263},{8... | collective-permute-start | bytes 1191944 | tf_op jit(solution)/shard_map/ppermute | solution.py:41
  63.3 29.2 %collective-permute-start.17 = (bf16[1552,128]{1,0:T(8,128)(2,1)S(1)}, bf16[1552,128]{1,0:T(8,128)(2,1)}, u32[]{:S(2)}, u32[]{:S(2)}) collective-permute-start(bf16[1552,128]{1,0:T(8,128)(2,1)S(1)} %collective-permute-done.6.refs_5_.refs_3_.refs_4_), channel_id=1, source_target_pairs={{1,24},{3,26},{5,28},{7,30},{8,0},{9,1},{10,2},{11,3},{12,4},{13,5... | collective-permute-start | bytes 1191944 | tf_op jit(solution)/shard_map/ppermute | solution.py:41
  65.3 0.8 copy-start
  66.0 29.4 %collective-permute-start.14 = (bf16[1552,128]{1,0:T(8,128)(2,1)S(1)}, bf16[1552,128]{1,0:T(8,128)(2,1)}, u32[]{:S(2)}, u32[]{:S(2)}) collective-permute-start(bf16[1552,128]{1,0:T(8,128)(2,1)S(1)} %collective-permute-done.6.refs_5_.refs_3_.refs_4_), channel_id=1, source_target_pairs={{0,8},{1,9},{2,10},{3,11},{4,12},{5,13},{6,14},{7,15},{8,16},{9,17... | collective-permute-start | bytes 1191944 | tf_op jit(solution)/shard_map/ppermute | solution.py:41
  72.4 0.8 copy-start.4
  73.2 16.2 %collective-permute-start.7 = (bf16[784,128]{1,0:T(8,128)(2,1)}, bf16[784,128]{1,0:T(8,128)(2,1)S(1)}, u32[]{:S(2)}, u32[]{:S(2)}) collective-permute-start(bf16[784,128]{1,0:T(8,128)(2,1)} %get-tuple-element.22), channel_id=1, source_target_pairs={{0,64},{1,160},{2,66},{3,162},{4,68},{5,164},{6,70},{7,166},{8,72}... | collective-permute-start | bytes 602120 | tf_op jit(solution)/shard_map/ppermute | solution.py:41
  75.1 30.1 %collective-permute-start.18 = (bf16[1552,128]{1,0:T(8,128)(2,1)}, bf16[1552,128]{1,0:T(8,128)(2,1)}, u32[]{:S(2)}, u32[]{:S(2)}) collective-permute-start(bf16[1552,128]{1,0:T(8,128)(2,1)} %collective-permute-done.12.refs_6_.refs_5_), channel_id=1, source_target_pairs={{1,24},{3,26},{5,28},{7,30},{8,0},{9,1},{10,2},{11,3},{12,4},{13,5... | collective-permute-start | bytes 1191944 | tf_op jit(solution)/shard_map/ppermute | solution.py:41
  77.1 28.2 %collective-permute-start.16 = (bf16[1552,128]{1,0:T(8,128)(2,1)}, bf16[1552,128]{1,0:T(8,128)(2,1)}, u32[]{:S(2)}, u32[]{:S(2)}) collective-permute-start(bf16[1552,128]{1,0:T(8,128)(2,1)} %collective-permute-done.12.refs_6_.refs_5_), channel_id=1, source_target_pairs={{0,8},{1,9},{2,10},{3,11},{4,12},{5,13},{6,14},{7,15},{8,16},{9,17... | collective-permute-start | bytes 1191944 | tf_op jit(solution)/shard_map/ppermute | solution.py:41
  81.7 12.8 %all-to-all-start = ((bf16[16,3,16,128]{3,2,1,0:T(8,128)(2,1)}), bf16[16,3,16,128]{3,2,1,0:T(8,128)(2,1)}, u32[]{:S(2)}, u32[]{:S(2)}) async-start(bf16[16,3,16,128]{3,2,1,0:T(8,128)(2,1)} %broadcast_in_dim.10), calls=%async_computation | async-start | bytes 393216 | tf_op jit(solution)/shard_map/all_to_all | solution.py:278
  89.4 5.1 %copy-start.8 = (bf16[784,128]{1,0:T(8,128)(2,1)}, bf16[784,128]{1,0:T(8,128)(2,1)S(1)}, u32[]{:S(2)}) copy-start(bf16[784,128]{1,0:T(8,128)(2,1)S(1)} %collective-permute-done.7.refs_0_) | copy-start | bytes 602116
  89.4 14.3 %collective-permute-start.5 = (bf16[784,128]{1,0:T(8,128)(2,1)}, bf16[784,128]{1,0:T(8,128)(2,1)}, u32[]{:S(2)}, u32[]{:S(2)}) collective-permute-start(bf16[784,128]{1,0:T(8,128)(2,1)} %get-tuple-element.20), channel_id=1, source_target_pairs={{0,32},{1,128},{2,34},{3,130},{4,36},{5,132},{6,38},{7,134},{8,40}... | collective-permute-start | bytes 602120 | tf_op jit(solution)/shard_map/ppermute | solution.py:41
  92.5 12.8 %collective-permute-start.11 = (bf16[784,128]{1,0:T(8,128)(2,1)}, bf16[784,128]{1,0:T(8,128)(2,1)}, u32[]{:S(2)}, u32[]{:S(2)}) collective-permute-start(bf16[784,128]{1,0:T(8,128)(2,1)} %get-tuple-element.24), channel_id=1, source_target_pairs={{64,64},{65,160},{66,66},{67,162},{68,68},{69,164},{70,70},{71,166... | collective-permute-start | bytes 602120 | tf_op jit(solution)/shard_map/ppermute | solution.py:41
  97.2 0.7 copy-start.7
  105.3 26.4 %all-to-all-start.1 = ((f32[16,16,256]{2,1,0:T(8,128)}), f32[16,16,256]{2,1,0:T(8,128)}, u32[]{:S(2)}, u32[]{:S(2)}) async-start(f32[16,16,256]{2,1,0:T(8,128)} %bitcast.43), calls=%async_computation.1 | async-start | bytes 524288 | tf_op jit(solution)/shard_map/all_to_all | solution.py:285
  116.4 1.0 copy-start.1
  117.4 1.0 copy-start.5
  130.3 0.7 copy-start.10
  131.0 0.7 copy-start.11
  134.8 24.3 %collective-permute-start.20 = (bf16[784,128]{1,0:T(8,128)(2,1)}, bf16[784,128]{1,0:T(8,128)(2,1)S(1)}, u32[]{:S(2)}, u32[]{:S(2)}) collective-permute-start(bf16[784,128]{1,0:T(8,128)(2,1)} %constant_dynamic-update-slice_fusion.10), channel_id=1, source_target_pairs={{0,64},{1,96},{2,66},{3,98},{4,68},{5,100},{6,70},{7,102},{8,72},{... | collective-permute-start | bytes 602120 | tf_op jit(solution)/shard_map/ppermute | solution.py:41
  137.5 21.5 %collective-permute-start.19 = (bf16[784,128]{1,0:T(8,128)(2,1)}, bf16[784,128]{1,0:T(8,128)(2,1)S(1)}, u32[]{:S(2)}, u32[]{:S(2)}) collective-permute-start(bf16[784,128]{1,0:T(8,128)(2,1)} %constant_dynamic-update-slice_fusion.11), channel_id=1, source_target_pairs={{0,0},{1,32},{2,2},{3,34},{4,4},{5,36},{6,6},{7,38},{8,8},{9,40},{... | collective-permute-start | bytes 602120 | tf_op jit(solution)/shard_map/ppermute | solution.py:41
  139.1 1.0 copy-start.2
  140.1 1.0 copy-start.6
  141.1 0.9 copy-start.9
  142.0 17.1 %copy-start.3 = (bf16[1552,128]{1,0:T(8,128)(2,1)S(1)}, bf16[1552,128]{1,0:T(8,128)(2,1)}, u32[]{:S(2)}) copy-start(bf16[1552,128]{1,0:T(8,128)(2,1)} %copy-done) | copy-start | bytes 1191940
  151.1 19.0 %collective-permute-start.21 = (bf16[784,128]{1,0:T(8,128)(2,1)}, bf16[784,128]{1,0:T(8,128)(2,1)}, u32[]{:S(2)}, u32[]{:S(2)}) collective-permute-start(bf16[784,128]{1,0:T(8,128)(2,1)} %constant_dynamic-update-slice_fusion.9), channel_id=1, source_target_pairs={{0,128},{1,160},{2,130},{3,162},{4,132},{5,164},{6,134},{7,166},{8... | collective-permute-start | bytes 602120 | tf_op jit(solution)/shard_map/ppermute | solution.py:41
  159.1 9.1 %copy-start.13 = (bf16[784,128]{1,0:T(8,128)(2,1)}, bf16[784,128]{1,0:T(8,128)(2,1)S(1)}, u32[]{:S(2)}) copy-start(bf16[784,128]{1,0:T(8,128)(2,1)S(1)} %collective-permute-done.20) | copy-start | bytes 602116
  159.1 9.0 %copy-start.14 = (bf16[784,128]{1,0:T(8,128)(2,1)}, bf16[784,128]{1,0:T(8,128)(2,1)S(1)}, u32[]{:S(2)}) copy-start(bf16[784,128]{1,0:T(8,128)(2,1)S(1)} %collective-permute-done.19) | copy-start | bytes 602116
  168.7 9.7 %collective-permute-start.22 = (bf16[784,128]{1,0:T(8,128)(2,1)}, bf16[784,128]{1,0:T(8,128)(2,1)S(1)}, u32[]{:S(2)}, u32[]{:S(2)}) collective-permute-start(bf16[784,128]{1,0:T(8,128)(2,1)} %constant_dynamic-update-slice_fusion.8), channel_id=1, source_target_pairs={{0,192},{1,224},{2,194},{3,226},{4,196},{5,228},{6,198},{7,230},{8... | collective-permute-start | bytes 602120 | tf_op jit(solution)/shard_map/ppermute | solution.py:41
  180.6 26.0 %all-to-all-start.2 = ((bf16[8,96,384]{2,1,0:T(8,128)(2,1)}), bf16[8,96,384]{2,1,0:T(8,128)(2,1)S(1)}, u32[]{:S(2)}, u32[]{:S(2)}) async-start(bf16[8,96,384]{2,1,0:T(8,128)(2,1)} %bitcast.15), calls=%async_computation.2 | async-start | bytes 1179648 | tf_op jit(solution)/shard_map/all_to_all | solution.py:302

commit v2 on v1

v2 whole, which is shorter than its diff:
```python
import functools
import math

import jax
import jax.numpy as jnp
import numpy as np
from jax import lax
from jax.experimental import pallas as pl
from jax.experimental.pallas import tpu as pltpu
from jax.sharding import Mesh
from jax.sharding import PartitionSpec as P


SIZES = (2, 8, 4, 4, 2)
NAMES = ("yl", "zr", "zp", "x", "yh", "c")
GROUP = ("yl", "x", "c")
HEAD = 128
TILE = 384
ROWS = 2 * TILE
SLOTS = 8
SHARE = ROWS // 8
CHUNK = SHARE + 16
BLOCK = 2 * ROWS + 16
RATE = math.log2(math.e) / math.sqrt(HEAD)
VMEM = 60 * 1024 * 1024
COST = pl.CostEstimate(flops=1 << 20, bytes_accessed=1 << 16, transcendentals=0)


def pairs_of(target):
    found = []
    for source in np.ndindex(*SIZES):
        aim = target(*source)
        if aim is not None:
            found.append(
                (int(np.ravel_multi_index(source, SIZES)), int(np.ravel_multi_index(aim, SIZES)))
            )
    return found


def send(value, target):
    return lax.ppermute(value, NAMES, pairs_of(target))


def to_column(turn):
    def target(yl, z, x, yh, c):
        i = (turn - z // 2) % 4
        return (yl, 4 * c + i, x, yh, z % 2) if i < 3 else None

    return target


def to_width(step):
    def target(yl, z, x, yh, c):
        width = 4 * c + x + step
        if z % 4 == 3 or not 0 <= width < 8:
            return None
        return (yl, z, width % 4, yh, width // 4)

    return target


def across(yl, z, x, yh, c):
    return (1 - yl, z, x, yh, c) if z % 4 < 3 else None


def dot_nt(a, b):
    return lax.dot_general(a, b, (((1,), (1,)), ((), ())), preferred_element_type=jnp.float32)


def fold_lanes(op, block):
    out = block[:, :HEAD]
    for start in range(HEAD, block.shape[1], HEAD):
        out = op(out, block[:, start : start + HEAD])
    return out


def weights_of(scores, peak):
    parts = []
    for start in range(0, scores.shape[1], HEAD):
        parts.append(jnp.exp2((scores[:, start : start + HEAD] - peak) * RATE))
    return functools.reduce(jnp.add, parts), jnp.concatenate(parts, axis=1).astype(jnp.bfloat16)


def column_kernel(params, lists, *refs):
    queries, blocks, (words, parts, out, pool, scores, sems) = refs[:4], refs[4:16], refs[16:]
    copies, start = [], 0
    for n, block in enumerate(blocks):
        place = pl.ds(start, block.shape[0])
        copies.append(pltpu.make_async_copy(block, pool.at[place], sems.at[n]))
        start += block.shape[0]
    for copy in copies:
        copy.start()
    yl, width, head, text_len = params[0], params[1], params[2], params[3]
    for copy in copies:
        copy.wait()
    row = lax.broadcasted_iota(jnp.int32, (TILE, 256), 1)
    live = text_token(row) < text_len

    def key_row(entry):
        height = (entry >> 4) - yl * 4
        turn = height + head
        slot = (turn & 1) * 2 + ((turn >> 1) & 1)
        slot = jnp.where((height >= 0) & (height < 4), slot, 4)
        shift = ((entry >> 1) & 7) - width
        slot = slot + jnp.where(shift == 0, 0, jnp.where(shift < 0, 5, 10))
        return jnp.clip(slot, 0, 14) * BLOCK + (entry & 1) * TILE

    text = merge_text(parts)
    for n in range(4):
        for yh in range(4):
            for c in range(2):
                out[c, n, yh, SHARE:, :] = text
    for turn in range(4):
        r = (turn - head) & 3
        found = []
        for half in range(2):
            base = (turn * 2 + half) * SLOTS
            rows, valid = [], []
            for j in range(SLOTS):
                entry = lists[base + j]
                valid.append(entry >= 0)
                rows.append(key_row(jnp.where(entry >= 0, entry, lists[base])))
            found.append((rows, valid))
        peaks = []
        for half, (rows, valid) in enumerate(found):
            q = queries[turn][half * TILE : (half + 1) * TILE, :]
            s = jnp.where(live, dot_nt(q, words[0]), -jnp.inf)
            scores[half, SLOTS, :, :256] = s
            peak = fold_lanes(jnp.maximum, s)
            for j in range(SLOTS):
                s = dot_nt(q, pool[pl.ds(pl.multiple_of(rows[j], 16), TILE), :])
                scores[half, j] = s
                s = fold_lanes(jnp.maximum, s)
                peak = jnp.maximum(peak, jnp.where(valid[j], s, -jnp.inf))
            peaks.append(jnp.max(peak, axis=1, keepdims=True))
        for half, (rows, valid) in enumerate(found):
            peak = jnp.broadcast_to(peaks[half], (TILE, HEAD))
            total, w = weights_of(scores[half, SLOTS, :, :256], peak)
            summed = jnp.dot(w, words[1], preferred_element_type=jnp.float32)
            for j in range(SLOTS):
                more, w = weights_of(scores[half, j], jnp.where(valid[j], peak, jnp.inf))
                total = total + more
                v = pool[pl.ds(pl.multiple_of(rows[j] + ROWS, 16), TILE), :]
                summed = summed + jnp.dot(w, v, preferred_element_type=jnp.float32)
            total = jnp.sum(total, axis=1, keepdims=True)
            done = (summed / total).astype(jnp.bfloat16)
            for n in range(4):
                out[n % 2, r, half * 2 + n // 2, :SHARE, :] = done[n * SHARE : (n + 1) * SHARE, :]


def attend_column(params, lists, queries, blocks, words, parts):
    smem = pl.BlockSpec(memory_space=pltpu.SMEM)
    vmem = pl.BlockSpec(memory_space=pltpu.VMEM)
    hbm = pl.BlockSpec(memory_space=pl.ANY)
    return pl.pallas_call(
        column_kernel,
        out_shape=jax.ShapeDtypeStruct((2, 4, 4, CHUNK, HEAD), jnp.bfloat16),
        in_specs=[smem, smem] + [vmem] * 4 + [hbm] * 12 + [vmem] * 2,
        out_specs=vmem,
        scratch_shapes=[
            pltpu.VMEM((15 * BLOCK, HEAD), jnp.bfloat16),
            pltpu.VMEM((2, SLOTS + 1, TILE, TILE), jnp.float32),
            pltpu.SemaphoreType.DMA((12,)),
        ],
        compiler_params=pltpu.CompilerParams(vmem_limit_bytes=VMEM),
        cost_estimate=COST,
        name="attend_column",
    )(params, lists, *queries, *blocks, words, parts)


def text_token(row):
    yl, x, z = row >> 7, (row >> 5) & 3, ((row >> 2) & 3) * 2 + ((row >> 4) & 1)
    return ((yl * 8 + z) * 4 + x) * 4 + (row & 3)


def stats_of(peak, total):
    lane = lax.broadcasted_iota(jnp.int32, (peak.shape[0], HEAD), 1)
    return jnp.where(lane == 0, peak, jnp.where(lane == 1, total, 0.0))


def text_kernel(limit, words, *refs):
    blocks, out = refs[:3], refs[3]
    row = lax.broadcasted_iota(jnp.int32, (256, 256), 1)
    q = words[0]
    scores, values = [], []
    for block in blocks:
        for start in range(0, block.shape[0], BLOCK):
            scores.append(dot_nt(q, block[start : start + ROWS, :]))
            values.append(block[start + ROWS : start + 2 * ROWS, :])
    scores.append(jnp.where(text_token(row) < limit[0], dot_nt(q, words[1]), -jnp.inf))
    values.append(words[2])
    peak = functools.reduce(jnp.maximum, [fold_lanes(jnp.maximum, s) for s in scores])
    peak = jnp.max(peak, axis=1, keepdims=True)
    total, summed = 0.0, 0.0
    for s, v in zip(scores, values):
        more, w = weights_of(s, peak)
        total = total + more
        summed = summed + jnp.dot(w, v, preferred_element_type=jnp.float32)
    stats = stats_of(peak, jnp.sum(total, axis=1, keepdims=True))
    out[:, :HEAD] = summed
    out[:, HEAD:] = stats


def attend_text(limit, words, blocks):
    vmem = pl.BlockSpec(memory_space=pltpu.VMEM)
    return pl.pallas_call(
        text_kernel,
        out_shape=jax.ShapeDtypeStruct((256, 256), jnp.float32),
        in_specs=[pl.BlockSpec(memory_space=pltpu.SMEM)] + [vmem] * 4,
        out_specs=vmem,
        compiler_params=pltpu.CompilerParams(vmem_limit_bytes=VMEM),
        cost_estimate=COST,
        name="attend_text",
    )(limit, words, *blocks)


def merge_text(parts):
    peak = functools.reduce(jnp.maximum, [parts[n, :, 128:129] for n in range(16)])
    total, summed = 0.0, 0.0
    for n in range(16):
        scale = jnp.exp2((parts[n, :, 128:129] - peak) * RATE)
        total = total + parts[n, :, 129:130] * scale
        summed = summed + parts[n, :, :HEAD] * scale
    return (summed / total).astype(jnp.bfloat16)


def after(value, *others):
    return lax.optimization_barrier((value, *others))[0]


def shards(q_video, k_video, v_video, q_text, k_text, v_text, tile_lists, text_len):
    yl, r, p, x, c = (lax.axis_index(name) for name in ("yl", "zr", "zp", "x", "c"))
    z = 2 * r + p
    head = z % 4

    def head_of(array, turn):
        i = jnp.minimum((turn - r) % 4, 2)
        return lax.dynamic_slice(array, (0, i * HEAD), (array.shape[0], HEAD))

    listed = jnp.pad(tile_lists.astype(jnp.bfloat16).reshape(1, 16), ((0, 3), (0, 112)))
    text = jnp.concatenate([q_text, k_text, v_text, jnp.tile(listed, (1, 3))], axis=0)
    own = {}
    for turn, behind in ((0, None), (2, None), (1, 0), (3, 2)):
        block = [head_of(array, turn) for array in (k_video, v_video, text)]
        block = jnp.concatenate(block, axis=0)
        if behind is not None:
            block = after(block, own[behind])
        own[turn] = send(block, to_column(turn))
    left, right = {}, {}
    for turn in (0, 2):
        left[turn], right[turn] = send(own[turn], to_width(1)), send(own[turn], to_width(-1))

    held = jnp.stack([own[turn][2 * ROWS :] for turn in range(4)])
    lists = held[:, 12, :16].astype(jnp.int32).reshape(64)
    held = lax.dynamic_slice(jnp.concatenate([held, held]), (head, 0, 0), (4, 12, HEAD))
    held = held.reshape(4, 3, 4, HEAD).transpose(1, 0, 2, 3).reshape(3, 16, HEAD)
    held = after(held, left[0], right[0], left[2], right[2])
    held = lax.all_to_all(jnp.broadcast_to(held, (16, 3, 16, HEAD)), GROUP, 0, 0, tiled=True)
    held = held.transpose(1, 0, 2, 3).reshape(3, 256, HEAD)

    edge = lax.select_n((jnp.where(yl == 0, 3, 0) + head) % 4, *(own[turn] for turn in range(4)))
    own[4] = send(edge, across)
    both = jnp.concatenate([own[1], own[3]], axis=0)
    left[1], right[1] = send(both, to_width(1)), send(both, to_width(-1))
    marks = (left[2], held, left[2], held)
    queries = [
        send(after(head_of(q_video, turn), mark), to_column(turn)) for turn, mark in enumerate(marks)
    ]

    first_column = (yl == 0) & (x == 0) & (c == 0)
    limit = jnp.where(first_column, text_len[0], 0).astype(jnp.int32)[None]
    held = after(held, queries[0], queries[2])
    packed = attend_text(limit, held, [own[0], own[2], both])
    edges = after(own[4], left[1], right[1])
    left[4], right[4] = send(edges, to_width(1)), send(edges, to_width(-1))
    packed = lax.all_to_all(packed.reshape(16, 16, 256), GROUP, 0, 0, tiled=True)

    blocks = [own[0], own[2], both, own[4], left[0], left[2], left[1], left[4]]
    blocks += [right[0], right[2], right[1], right[4]]

    params = jnp.stack([yl, 4 * c + x, head, text_len[0]]).astype(jnp.int32)
    done = attend_column(params, lists, queries, blocks, held[1:], packed)
    done = lax.all_to_all(done, "c", 0, 0, tiled=True)
    done = lax.all_to_all(done.reshape(32, CHUNK, HEAD), ("zp", "zr", "yh"), 0, 0, tiled=True)
    done = done.reshape(2, 4, 4, CHUNK, HEAD).transpose(3, 2, 1, 0, 4).reshape(CHUNK, 4, 2, 4, HEAD)
    video_out = done[:SHARE, :, :, :3].reshape(SHARE, 24 * HEAD)
    yh = lax.axis_index("yh")
    text_out = lax.dynamic_slice(done, (SHARE + 4 * r, yh, c, 0, 0), (4, 1, 1, 3, HEAD))
    return (video_out, text_out.reshape(4, 3 * HEAD))


def solution(mesh):
    fine = Mesh(mesh.devices.reshape(2, 4, 2, 4, 4, 2), NAMES)
    tile, head = ("yl", "zr", "zp", "x"), ("yh", "c")
    split = P(tile, head)
    in_specs = (split,) * 6 + (P(tile, None), P())
    out_specs = (P(tile + head, None), split)
    return jax.shard_map(shards, mesh=fine, in_specs=in_specs, out_specs=out_specs, check_vma=False)
```

time: 209 us -> 191 us (0.914)
  the two profiles are of different devices: /device:TPU:2 before, /device:TPU:8 now
where the time goes in v2:
time: 191 us; the launch traced here: 189 us
  starting transfers between devices  76 us (40%)
  waiting for transfers between devices  64.2 us (34%)
  Pallas kernels  23.2 us (12%)
  local copies, waits for them, and re-layouts  14.5 us (8%)
  blocking collectives  7.59 us (4%)
  between operations  1.93 us (1%)
    ppermute x17, starting transfers between devices, send(): return lax.ppermute(value, NAMES, pairs_of(target))  45.9 us
    all_to_all x1, waiting for transfers between devices, shards(): lax.all_to_all(done.reshape(32, CHUNK, HEAD), ('zp', 'zr', 'yh'), 0, 0, t...  32.8 us
    ppermute x17, waiting for transfers between devices, send(): return lax.ppermute(value, NAMES, pairs_of(target))  26.8 us
    pallas_call x1, Pallas kernels, attend_column(): pl.pallas_call(column_kernel, out_shape=jax.ShapeDtypeStruct((2, 4, 4, CH...  19.4 us
    all_to_all x1, starting transfers between devices, shards(): lax.all_to_all(jnp.broadcast_to(held, (16, 3, 16, HEAD)), GROUP, 0, 0, ti...  14.3 us
    all_to_all x1, starting transfers between devices, shards(): lax.all_to_all(done.reshape(32, CHUNK, HEAD), ('zp', 'zr', 'yh'), 0, 0, t...  8.99 us
    all_to_all x1, blocking collectives, shards(): done = lax.all_to_all(done, 'c', 0, 0, tiled=True)  7.59 us
    all_to_all x1, starting transfers between devices, shards(): lax.all_to_all(packed.reshape(16, 16, 256), GROUP, 0, 0, tiled=True)  6.92 us
  transfers between devices with their start and end apart: 20, of which 7 were waited for; matrix products, arithmetic and copies ran while one was open for 4% of the time, Pallas kernels for 2%

profile of v2, /device:TPU:8, one launch (start us, length us, event | category | flops | bytes accessed | tf_op | source)
XLA Modules:
  0.0 189.3 jit_solution(12431919156368522318)
XLA Ops:
  0.7 0.7 copy-done.22
  1.4 0.1 reshape.42
  1.5 0.0 copy-start.20
  1.5 0.0 copy-start.19
  1.5 0.6 copy-done.21
  2.2 0.0 copy-done.20
  2.2 0.0 copy-done.19
  2.2 1.6 constant_dynamic-slice_fusion.16
  3.9 6.1 %collective-permute-start.2 = (bf16[1552,128]{1,0:T(8,128)(2,1)S(1)}, bf16[1552,128]{1,0:T(8,128)(2,1)S(1)}, u32[]{:S(2)}, u32[]{:S(2)}) collective-permute-start(bf16[1552,128]{1,0:T(8,128)(2,1)S(1)} %pad_maximum_fusion.2), channel_id=1, source_target_pairs={{0,64},{1,192},{2,66},{3,194},{4,68},{5,196},{6,70},{7,198},{8,72}... | collective-permute-start | bytes 1191944 | tf_op jit(solution)/shard_map/ppermute | solution.py:41
  10.0 0.7 collective-permute-start
  10.8 16.6 %collective-permute-done.2.refs_1_.refs_5_ = bf16[1552,128]{1,0:T(8,128)(2,1)S(1)} collective-permute-done((bf16[1552,128]{1,0:T(8,128)(2,1)S(1)}, bf16[1552,128]{1,0:T(8,128)(2,1)S(1)}, u32[]{:S(2)}, u32[]{:S(2)}) %collective-permute-start.2) | collective-permute-done | bytes 397344 | tf_op jit(solution)/shard_map/ppermute | solution.py:41
  27.4 1.3 collective-permute-start.3
  28.7 2.2 %collective-permute-start.1 = (bf16[1552,128]{1,0:T(8,128)(2,1)S(1)}, bf16[1552,128]{1,0:T(8,128)(2,1)S(1)}, u32[]{:S(2)}, u32[]{:S(2)}) collective-permute-start(bf16[1552,128]{1,0:T(8,128)(2,1)S(1)} %pad_maximum_fusion.1), channel_id=1, source_target_pairs={{0,32},{1,160},{2,34},{3,162},{4,36},{5,164},{6,38},{7,166},{8,40}... | collective-permute-start | bytes 1191944 | tf_op jit(solution)/shard_map/ppermute | solution.py:41
  31.6 1.3 collective-permute-start.8
  32.9 4.6 %collective-permute-start.4 = (bf16[1552,128]{1,0:T(8,128)(2,1)S(1)}, bf16[1552,128]{1,0:T(8,128)(2,1)S(1)}, u32[]{:S(2)}, u32[]{:S(2)}) collective-permute-start(bf16[1552,128]{1,0:T(8,128)(2,1)S(1)} %collective-permute-done.2.refs_1_.refs_5_), channel_id=1, source_target_pairs={{0,8},{1,9},{2,10},{3,11},{4,12},{5,13},{6,14},{7,15},{8,16},{9,17... | collective-permute-start | bytes 1191944 | tf_op jit(solution)/shard_map/ppermute | solution.py:41
  37.5 1.3 collective-permute-start.7
  38.8 0.4 collective-permute-done.3
  39.2 4.2 %collective-permute-start.6 = (bf16[1552,128]{1,0:T(8,128)(2,1)S(1)}, bf16[1552,128]{1,0:T(8,128)(2,1)S(1)}, u32[]{:S(2)}, u32[]{:S(2)}) collective-permute-start(bf16[1552,128]{1,0:T(8,128)(2,1)S(1)} %collective-permute-done.refs_0_.refs_4_), channel_id=1, source_target_pairs={{0,8},{1,9},{2,10},{3,11},{4,12},{5,13},{6,14},{7,15},{8,16},{9,17... | collective-permute-start | bytes 1191944 | tf_op jit(solution)/shard_map/ppermute | solution.py:41
  43.4 0.0 copy-start.7
  43.4 1.0 select_select_fusion
  44.4 0.1 constant_dynamic-update-slice_fusion.8.refs_2_.refs_6_
  44.5 1.4 collective-permute-start.14
  45.9 0.7 constant_dynamic-update-slice_fusion.6
  46.6 0.7 constant_dynamic-update-slice_fusion.2
  47.4 0.0 collective-permute-done.8.refs_13_
  47.4 5.4 %collective-permute-start.13 = (bf16[3104,128]{1,0:T(8,128)(2,1)S(1)}, bf16[3104,128]{1,0:T(8,128)(2,1)}, u32[]{:S(2)}, u32[]{:S(2)}) collective-permute-start(bf16[3104,128]{1,0:T(8,128)(2,1)S(1)} %constant_dynamic-update-slice_fusion.8.refs_2_.refs_6_), channel_id=1, source_target_pairs={{0,8},{1,9},{2,10},{3,11},{4,12},{5,13},{6,14},{7,15},{8,16},{9,17... | collective-permute-start | bytes 2383880 | tf_op jit(solution)/shard_map/ppermute | solution.py:41
  52.8 0.0 collective-permute-done.7.refs_12_
  52.9 0.7 copy-done.9
  53.6 0.2 copy-done.10
  53.8 0.2 copy-done.11
  53.9 0.7 broadcast_in_dim.6
  54.6 14.3 %all-to-all-start = ((bf16[16,3,16,128]{3,2,1,0:T(8,128)(2,1)}), bf16[16,3,16,128]{3,2,1,0:T(8,128)(2,1)S(1)}, u32[]{:S(2)}, u32[]{:S(2)}) async-start(bf16[16,3,16,128]{3,2,1,0:T(8,128)(2,1)} %broadcast_in_dim.6), calls=%async_computation | async-start | bytes 393216 | tf_op jit(solution)/shard_map/all_to_all | solution.py:258
  68.9 0.6 pad_add_fusion.params
  69.5 0.9 constant_dynamic-slice_fusion.1
  70.4 1.6 collective-permute-start.5
  72.0 2.1 %collective-permute-start.10 = (bf16[768,128]{1,0:T(8,128)(2,1)}, bf16[768,128]{1,0:T(8,128)(2,1)}, u32[]{:S(2)}, u32[]{:S(2)}) collective-permute-start(bf16[768,128]{1,0:T(8,128)(2,1)} %get-tuple-element.16), channel_id=1, source_target_pairs={{0,64},{1,192},{2,66},{3,194},{4,68},{5,196},{6,70},{7,198},{8,72}... | collective-permute-start | bytes 589832 | tf_op jit(solution)/shard_map/ppermute | solution.py:41
  74.1 2.0 %collective-permute-start.12 = (bf16[1552,128]{1,0:T(8,128)(2,1)}, bf16[1552,128]{1,0:T(8,128)(2,1)S(1)}, u32[]{:S(2)}, u32[]{:S(2)}) collective-permute-start(bf16[1552,128]{1,0:T(8,128)(2,1)} %get-tuple-element.32), channel_id=1, source_target_pairs={{0,256},{1,257},{2,258},{3,259},{4,260},{5,261},{6,262},{7,263},{8... | collective-permute-start | bytes 1191944 | tf_op jit(solution)/shard_map/ppermute | solution.py:41
  76.2 4.6 %all-to-all-done = bf16[16,3,16,128]{3,2,1,0:T(8,128)(2,1)S(1)} async-done(((bf16[16,3,16,128]{3,2,1,0:T(8,128)(2,1)}), bf16[16,3,16,128]{3,2,1,0:T(8,128)(2,1)S(1)}, u32[]{:S(2)}, u32[]{:S(2)}) %all-to-all-start) | async-done | bytes 196640 | tf_op jit(solution)/shard_map/all_to_all | solution.py:258
  80.8 0.7 copy.19
  81.5 3.4 %collective-permute-done.10.refs_2_ = bf16[768,128]{1,0:T(8,128)(2,1)} collective-permute-done((bf16[768,128]{1,0:T(8,128)(2,1)}, bf16[768,128]{1,0:T(8,128)(2,1)}, u32[]{:S(2)}, u32[]{:S(2)}) %collective-permute-start.10) | collective-permute-done | bytes 196640 | tf_op jit(solution)/shard_map/ppermute | solution.py:41
  84.9 3.8 %attend_text.1 = f32[256,256]{1,0:T(8,128)} custom-call(s32[1]{0:T(128)} %bitcast.14.limit, bf16[3,256,128]{2,1,0:T(8,128)(2,1)} %bitcast.49, bf16[1552,128]{1,0:T(8,128)(2,1)} %copy-done.2, bf16[1552,128]{1,0:T(8,128)(2,1)} %copy-done.1, bf16[3104,128]{1,0:T(8,128)(2,1)} %copy-done), custom_call_target="tpu_custom_call" | custom-call | flops 1048576 | bytes 65536 | tf_op jit(solution)/shard_map/attend_text/pallas_call | solution.py:206
  88.8 6.9 %all-to-all-start.1 = ((f32[16,16,256]{2,1,0:T(8,128)}), f32[16,16,256]{2,1,0:T(8,128)S(1)}, u32[]{:S(2)}, u32[]{:S(2)}) async-start(f32[16,16,256]{2,1,0:T(8,128)} %bitcast.51), calls=%async_computation.1 | async-start | bytes 524288 | tf_op jit(solution)/shard_map/all_to_all | solution.py:276
  95.7 0.7 slice_bitcast_fusion.3
  96.4 1.3 collective-permute-start.16
  97.7 4.6 %collective-permute-start.15 = (bf16[1552,128]{1,0:T(8,128)(2,1)S(1)}, bf16[1552,128]{1,0:T(8,128)(2,1)S(1)}, u32[]{:S(2)}, u32[]{:S(2)}) collective-permute-start(bf16[1552,128]{1,0:T(8,128)(2,1)S(1)} %collective-permute-done.12.refs_7_), channel_id=1, source_target_pairs={{0,8},{1,9},{2,10},{3,11},{4,12},{5,13},{6,14},{7,15},{8,16},{9,17... | collective-permute-start | bytes 1191944 | tf_op jit(solution)/shard_map/ppermute | solution.py:41
  102.3 4.4 %collective-permute-start.9 = (bf16[768,128]{1,0:T(8,128)(2,1)S(1)}, bf16[768,128]{1,0:T(8,128)(2,1)S(1)}, u32[]{:S(2)}, u32[]{:S(2)}) collective-permute-start(bf16[768,128]{1,0:T(8,128)(2,1)S(1)} %copy-done.15), channel_id=1, source_target_pairs={{0,32},{1,160},{2,34},{3,162},{4,36},{5,164},{6,38},{7,166},{8,40}... | collective-permute-start | bytes 589832 | tf_op jit(solution)/shard_map/ppermute | solution.py:41
  106.7 1.5 collective-permute-start.11
  108.2 0.7 slice_bitcast_fusion.2
  108.9 0.6 reshape.52.lists
  109.5 0.7 slice.26.refs_16_
  110.2 2.9 %collective-permute-done.9.refs_1_ = bf16[768,128]{1,0:T(8,128)(2,1)S(1)} collective-permute-done((bf16[768,128]{1,0:T(8,128)(2,1)S(1)}, bf16[768,128]{1,0:T(8,128)(2,1)S(1)}, u32[]{:S(2)}, u32[]{:S(2)}) %collective-permute-start.9) | collective-permute-done | bytes 196640 | tf_op jit(solution)/shard_map/ppermute | solution.py:41
  113.1 3.4 %collective-permute-done.11.refs_3_ = bf16[768,128]{1,0:T(8,128)(2,1)S(1)} collective-permute-done((bf16[768,128]{1,0:T(8,128)(2,1)S(1)}, bf16[768,128]{1,0:T(8,128)(2,1)S(1)}, u32[]{:S(2)}, u32[]{:S(2)}) %collective-permute-start.11) | collective-permute-done | bytes 196640 | tf_op jit(solution)/shard_map/ppermute | solution.py:41
  116.6 0.6 copy-done.18
  117.2 0.1 copy-done.4
  117.3 0.1 copy-done.13
  117.4 0.7 copy-done.14
  118.2 19.4 %attend_column.1 = bf16[2,4,4,112,128]{4,3,2,1,0:T(8,128)(2,1)} custom-call(s32[4]{0:T(128)} %pad_add_fusion.params, s32[64]{0:T(128)} %reshape.52.lists, bf16[768,128]{1,0:T(8,128)(2,1)} %copy-done.16, bf16[768,128]{1,0:T(8,128)(2,1)} %copy-done.17, bf16[768,128]{1,0:T(8,128)(2,1)} %collective-permute-done.10.refs_2_, bf16[768,128]{1,0:T(8,128)(2,1)} %copy-done.18, ...), custom_call_target="tpu_custom_call" | custom-call | flops 1048576 | bytes 65536 | tf_op jit(solution)/shard_map/attend_column/pallas_call | solution.py:155
  137.5 7.6 %all_to_all.20 = bf16[2,4,4,112,128]{4,3,2,1,0:T(8,128)(2,1)} all-to-all(bf16[2,4,4,112,128]{4,3,2,1,0:T(8,128)(2,1)} %attend_column.1), channel_id=1, replica_groups=mesh['yl'=2,'zr'=4,'zp'=2,'x'=4,'yh'=4,'c'=2] {'c'}, dimensions={0} | all-to-all | bytes 1835008 | tf_op jit(solution)/shard_map/all_to_all | solution.py:283
  145.1 9.0 %all-to-all-start.3 = ((bf16[32,112,128]{2,1,0:T(8,128)(2,1)}), bf16[32,112,128]{2,1,0:T(8,128)(2,1)S(1)}, u32[]{:S(2)}, u32[]{:S(2)}) async-start(bf16[32,112,128]{2,1,0:T(8,128)(2,1)} %bitcast.16), calls=%async_computation.3 | async-start | bytes 1835008 | tf_op jit(solution)/shard_map/all_to_all | solution.py:284
  154.1 32.8 %all-to-all-done.3 = bf16[32,112,128]{2,1,0:T(8,128)(2,1)S(1)} async-done(((bf16[32,112,128]{2,1,0:T(8,128)(2,1)}), bf16[32,112,128]{2,1,0:T(8,128)(2,1)S(1)}, u32[]{:S(2)}, u32[]{:S(2)}) %all-to-all-start.3) | async-done | bytes 917536 | tf_op jit(solution)/shard_map/all_to_all | solution.py:284
  186.9 0.1 copy.20
  187.0 0.4 copy.21
  187.4 1.2 reshape.50
  188.7 0.6 fusion
  (65 shorter events, 0.4 us)
Async XLA Ops:
  0.7 0.7 copy-start.22
  1.5 0.7 copy-start.21
  1.5 0.7 copy-start.20
  1.5 0.7 copy-start.19
  3.9 23.5 %collective-permute-start.2 = (bf16[1552,128]{1,0:T(8,128)(2,1)S(1)}, bf16[1552,128]{1,0:T(8,128)(2,1)S(1)}, u32[]{:S(2)}, u32[]{:S(2)}) collective-permute-start(bf16[1552,128]{1,0:T(8,128)(2,1)S(1)} %pad_maximum_fusion.2), channel_id=1, source_target_pairs={{0,64},{1,192},{2,66},{3,194},{4,68},{5,196},{6,70},{7,198},{8,72}... | collective-permute-start | bytes 1191944 | tf_op jit(solution)/shard_map/ppermute | solution.py:41
  10.0 18.7 %collective-permute-start = (bf16[1552,128]{1,0:T(8,128)(2,1)S(1)}, bf16[1552,128]{1,0:T(8,128)(2,1)S(1)}, u32[]{:S(2)}, u32[]{:S(2)}) collective-permute-start(bf16[1552,128]{1,0:T(8,128)(2,1)S(1)} %pad_maximum_fusion), channel_id=1, source_target_pairs={{0,0},{1,128},{2,2},{3,130},{4,4},{5,132},{6,6},{7,134},{8,8},{9,1... | collective-permute-start | bytes 1191944 | tf_op jit(solution)/shard_map/ppermute | solution.py:41
  27.4 48.7 %copy-start.1 = (bf16[1552,128]{1,0:T(8,128)(2,1)}, bf16[1552,128]{1,0:T(8,128)(2,1)S(1)}, u32[]{:S(2)}) copy-start(bf16[1552,128]{1,0:T(8,128)(2,1)S(1)} %collective-permute-done.2.refs_1_.refs_5_) | copy-start | bytes 1191940
  27.4 11.8 %collective-permute-start.3 = (bf16[1552,128]{1,0:T(8,128)(2,1)S(1)}, bf16[1552,128]{1,0:T(8,128)(2,1)S(1)}, u32[]{:S(2)}, u32[]{:S(2)}) collective-permute-start(bf16[1552,128]{1,0:T(8,128)(2,1)S(1)} %pad_maximum_fusion.3), channel_id=1, source_target_pairs={{64,64},{65,192},{66,66},{67,194},{68,68},{69,196},{70,70},{71,198... | collective-permute-start | bytes 1191944 | tf_op jit(solution)/shard_map/ppermute | solution.py:41
  28.7 17.9 %copy-start.2 = (bf16[1552,128]{1,0:T(8,128)(2,1)}, bf16[1552,128]{1,0:T(8,128)(2,1)S(1)}, u32[]{:S(2)}) copy-start(bf16[1552,128]{1,0:T(8,128)(2,1)S(1)} %collective-permute-done.refs_0_.refs_4_) | copy-start | bytes 1191940
  28.7 14.7 %collective-permute-start.1 = (bf16[1552,128]{1,0:T(8,128)(2,1)S(1)}, bf16[1552,128]{1,0:T(8,128)(2,1)S(1)}, u32[]{:S(2)}, u32[]{:S(2)}) collective-permute-start(bf16[1552,128]{1,0:T(8,128)(2,1)S(1)} %pad_maximum_fusion.1), channel_id=1, source_target_pairs={{0,32},{1,160},{2,34},{3,162},{4,36},{5,164},{6,38},{7,166},{8,40}... | collective-permute-start | bytes 1191944 | tf_op jit(solution)/shard_map/ppermute | solution.py:41
  31.6 15.7 %collective-permute-start.8 = (bf16[1552,128]{1,0:T(8,128)(2,1)S(1)}, bf16[1552,128]{1,0:T(8,128)(2,1)S(1)}, u32[]{:S(2)}, u32[]{:S(2)}) collective-permute-start(bf16[1552,128]{1,0:T(8,128)(2,1)S(1)} %collective-permute-done.2.refs_1_.refs_5_), channel_id=1, source_target_pairs={{1,24},{3,26},{5,28},{7,30},{8,0},{9,1},{10,2},{11,3},{12,4},{13,5... | collective-permute-start | bytes 1191944 | tf_op jit(solution)/shard_map/ppermute | solution.py:41
  32.9 19.9 %collective-permute-start.4 = (bf16[1552,128]{1,0:T(8,128)(2,1)S(1)}, bf16[1552,128]{1,0:T(8,128)(2,1)S(1)}, u32[]{:S(2)}, u32[]{:S(2)}) collective-permute-start(bf16[1552,128]{1,0:T(8,128)(2,1)S(1)} %collective-permute-done.2.refs_1_.refs_5_), channel_id=1, source_target_pairs={{0,8},{1,9},{2,10},{3,11},{4,12},{5,13},{6,14},{7,15},{8,16},{9,17... | collective-permute-start | bytes 1191944 | tf_op jit(solution)/shard_map/ppermute | solution.py:41
  37.5 15.4 %collective-permute-start.7 = (bf16[1552,128]{1,0:T(8,128)(2,1)S(1)}, bf16[1552,128]{1,0:T(8,128)(2,1)S(1)}, u32[]{:S(2)}, u32[]{:S(2)}) collective-permute-start(bf16[1552,128]{1,0:T(8,128)(2,1)S(1)} %collective-permute-done.refs_0_.refs_4_), channel_id=1, source_target_pairs={{1,24},{3,26},{5,28},{7,30},{8,0},{9,1},{10,2},{11,3},{12,4},{13,5... | collective-permute-start | bytes 1191944 | tf_op jit(solution)/shard_map/ppermute | solution.py:41
  39.2 13.6 %collective-permute-start.6 = (bf16[1552,128]{1,0:T(8,128)(2,1)S(1)}, bf16[1552,128]{1,0:T(8,128)(2,1)S(1)}, u32[]{:S(2)}, u32[]{:S(2)}) collective-permute-start(bf16[1552,128]{1,0:T(8,128)(2,1)S(1)} %collective-permute-done.refs_0_.refs_4_), channel_id=1, source_target_pairs={{0,8},{1,9},{2,10},{3,11},{4,12},{5,13},{6,14},{7,15},{8,16},{9,17... | collective-permute-start | bytes 1191944 | tf_op jit(solution)/shard_map/ppermute | solution.py:41
  43.4 1.0 copy-start.7
  44.4 25.1 %copy-start.5 = (bf16[768,384]{1,0:T(8,128)(2,1)S(1)}, bf16[768,384]{1,0:T(8,128)(2,1)}, u32[]{:S(2)}) copy-start(bf16[768,384]{1,0:T(8,128)(2,1)} %param.8) | copy-start | bytes 1769476
  44.5 25.9 %copy-start = (bf16[3104,128]{1,0:T(8,128)(2,1)}, bf16[3104,128]{1,0:T(8,128)(2,1)S(1)}, u32[]{:S(2)}) copy-start(bf16[3104,128]{1,0:T(8,128)(2,1)S(1)} %constant_dynamic-update-slice_fusion.8.refs_2_.refs_6_) | copy-start | bytes 2383876
  44.5 51.9 %collective-permute-start.14 = (bf16[3104,128]{1,0:T(8,128)(2,1)S(1)}, bf16[3104,128]{1,0:T(8,128)(2,1)S(1)}, u32[]{:S(2)}, u32[]{:S(2)}) collective-permute-start(bf16[3104,128]{1,0:T(8,128)(2,1)S(1)} %constant_dynamic-update-slice_fusion.8.refs_2_.refs_6_), channel_id=1, source_target_pairs={{1,24},{3,26},{5,28},{7,30},{8,0},{9,1},{10,2},{11,3},{12,4},{13,5... | collective-permute-start | bytes 2383880 | tf_op jit(solution)/shard_map/ppermute | solution.py:41
  47.4 5.5 %copy-start.8 = (bf16[1552,128]{1,0:T(8,128)(2,1)}, bf16[1552,128]{1,0:T(8,128)(2,1)S(1)}, u32[]{:S(2)}) copy-start(bf16[1552,128]{1,0:T(8,128)(2,1)S(1)} %collective-permute-done.8.refs_13_) | copy-start | bytes 1191940
  47.4 49.0 %collective-permute-start.13 = (bf16[3104,128]{1,0:T(8,128)(2,1)S(1)}, bf16[3104,128]{1,0:T(8,128)(2,1)}, u32[]{:S(2)}, u32[]{:S(2)}) collective-permute-start(bf16[3104,128]{1,0:T(8,128)(2,1)S(1)} %constant_dynamic-update-slice_fusion.8.refs_2_.refs_6_), channel_id=1, source_target_pairs={{0,8},{1,9},{2,10},{3,11},{4,12},{5,13},{6,14},{7,15},{8,16},{9,17... | collective-permute-start | bytes 2383880 | tf_op jit(solution)/shard_map/ppermute | solution.py:41
  52.8 0.8 copy-start.9
  52.9 0.9 copy-start.10
  52.9 1.0 copy-start.11
  54.6 26.2 %all-to-all-start = ((bf16[16,3,16,128]{3,2,1,0:T(8,128)(2,1)}), bf16[16,3,16,128]{3,2,1,0:T(8,128)(2,1)S(1)}, u32[]{:S(2)}, u32[]{:S(2)}) async-start(bf16[16,3,16,128]{3,2,1,0:T(8,128)(2,1)} %broadcast_in_dim.6), calls=%async_computation | async-start | bytes 393216 | tf_op jit(solution)/shard_map/all_to_all | solution.py:258
  70.4 11.1 %collective-permute-start.5 = (bf16[768,128]{1,0:T(8,128)(2,1)}, bf16[768,128]{1,0:T(8,128)(2,1)S(1)}, u32[]{:S(2)}, u32[]{:S(2)}) collective-permute-start(bf16[768,128]{1,0:T(8,128)(2,1)} %get-tuple-element.13), channel_id=1, source_target_pairs={{0,0},{1,128},{2,2},{3,130},{4,4},{5,132},{6,6},{7,134},{8,8},{9,1... | collective-permute-start | bytes 589832 | tf_op jit(solution)/shard_map/ppermute | solution.py:41
  72.0 12.9 %collective-permute-start.10 = (bf16[768,128]{1,0:T(8,128)(2,1)}, bf16[768,128]{1,0:T(8,128)(2,1)}, u32[]{:S(2)}, u32[]{:S(2)}) collective-permute-start(bf16[768,128]{1,0:T(8,128)(2,1)} %get-tuple-element.16), channel_id=1, source_target_pairs={{0,64},{1,192},{2,66},{3,194},{4,68},{5,196},{6,70},{7,198},{8,72}... | collective-permute-start | bytes 589832 | tf_op jit(solution)/shard_map/ppermute | solution.py:41
  74.1 22.2 %collective-permute-start.12 = (bf16[1552,128]{1,0:T(8,128)(2,1)}, bf16[1552,128]{1,0:T(8,128)(2,1)S(1)}, u32[]{:S(2)}, u32[]{:S(2)}) collective-permute-start(bf16[1552,128]{1,0:T(8,128)(2,1)} %get-tuple-element.32), channel_id=1, source_target_pairs={{0,256},{1,257},{2,258},{3,259},{4,260},{5,261},{6,262},{7,263},{8... | collective-permute-start | bytes 1191944 | tf_op jit(solution)/shard_map/ppermute | solution.py:41
  81.5 7.3 %copy-start.16 = (bf16[768,128]{1,0:T(8,128)(2,1)}, bf16[768,128]{1,0:T(8,128)(2,1)S(1)}, u32[]{:S(2)}) copy-start(bf16[768,128]{1,0:T(8,128)(2,1)S(1)} %collective-permute-done.5.refs_0_) | copy-start | bytes 589828
  88.8 13.5 %copy-start.15 = (bf16[768,128]{1,0:T(8,128)(2,1)S(1)}, bf16[768,128]{1,0:T(8,128)(2,1)}, u32[]{:S(2)}) copy-start(bf16[768,128]{1,0:T(8,128)(2,1)} %get-tuple-element.15) | copy-start | bytes 589828
  88.8 20.7 %copy-start.3 = (bf16[3,16,16,128]{3,2,1,0:T(8,128)(2,1)S(1)}, bf16[3,16,16,128]{3,2,1,0:T(8,128)(2,1)}, u32[]{:S(2)}) copy-start(bf16[3,16,16,128]{3,2,1,0:T(8,128)(2,1)} %copy.19) | copy-start | bytes 589828
  88.8 27.7 %all-to-all-start.1 = ((f32[16,16,256]{2,1,0:T(8,128)}), f32[16,16,256]{2,1,0:T(8,128)S(1)}, u32[]{:S(2)}, u32[]{:S(2)}) async-start(f32[16,16,256]{2,1,0:T(8,128)} %bitcast.51), calls=%async_computation.1 | async-start | bytes 524288 | tf_op jit(solution)/shard_map/all_to_all | solution.py:276
  96.4 20.2 %copy-start.12 = (bf16[1552,128]{1,0:T(8,128)(2,1)}, bf16[1552,128]{1,0:T(8,128)(2,1)S(1)}, u32[]{:S(2)}) copy-start(bf16[1552,128]{1,0:T(8,128)(2,1)S(1)} %collective-permute-done.12.refs_7_) | copy-start | bytes 1191940
  96.4 20.2 %copy-start.6 = (bf16[3104,128]{1,0:T(8,128)(2,1)}, bf16[3104,128]{1,0:T(8,128)(2,1)S(1)}, u32[]{:S(2)}) copy-start(bf16[3104,128]{1,0:T(8,128)(2,1)S(1)} %collective-permute-done.14.refs_14_) | copy-start | bytes 2383876
  96.4 20.1 %collective-permute-start.16 = (bf16[1552,128]{1,0:T(8,128)(2,1)S(1)}, bf16[1552,128]{1,0:T(8,128)(2,1)S(1)}, u32[]{:S(2)}, u32[]{:S(2)}) collective-permute-start(bf16[1552,128]{1,0:T(8,128)(2,1)S(1)} %collective-permute-done.12.refs_7_), channel_id=1, source_target_pairs={{1,24},{3,26},{5,28},{7,30},{8,0},{9,1},{10,2},{11,3},{12,4},{13,5... | collective-permute-start | bytes 1191944 | tf_op jit(solution)/shard_map/ppermute | solution.py:41
  97.7 18.8 %collective-permute-start.15 = (bf16[1552,128]{1,0:T(8,128)(2,1)S(1)}, bf16[1552,128]{1,0:T(8,128)(2,1)S(1)}, u32[]{:S(2)}, u32[]{:S(2)}) collective-permute-start(bf16[1552,128]{1,0:T(8,128)(2,1)S(1)} %collective-permute-done.12.refs_7_), channel_id=1, source_target_pairs={{0,8},{1,9},{2,10},{3,11},{4,12},{5,13},{6,14},{7,15},{8,16},{9,17... | collective-permute-start | bytes 1191944 | tf_op jit(solution)/shard_map/ppermute | solution.py:41
  102.3 10.8 %collective-permute-start.9 = (bf16[768,128]{1,0:T(8,128)(2,1)S(1)}, bf16[768,128]{1,0:T(8,128)(2,1)S(1)}, u32[]{:S(2)}, u32[]{:S(2)}) collective-permute-start(bf16[768,128]{1,0:T(8,128)(2,1)S(1)} %copy-done.15), channel_id=1, source_target_pairs={{0,32},{1,160},{2,34},{3,162},{4,36},{5,164},{6,38},{7,166},{8,40}... | collective-permute-start | bytes 589832 | tf_op jit(solution)/shard_map/ppermute | solution.py:41
  106.7 9.8 %collective-permute-start.11 = (bf16[768,128]{1,0:T(8,128)(2,1)S(1)}, bf16[768,128]{1,0:T(8,128)(2,1)S(1)}, u32[]{:S(2)}, u32[]{:S(2)}) collective-permute-start(bf16[768,128]{1,0:T(8,128)(2,1)S(1)} %get-tuple-element.17), channel_id=1, source_target_pairs={{64,64},{65,192},{66,66},{67,194},{68,68},{69,196},{70,70},{71,198... | collective-permute-start | bytes 589832 | tf_op jit(solution)/shard_map/ppermute | solution.py:41
  113.1 3.5 %copy-start.17 = (bf16[768,128]{1,0:T(8,128)(2,1)}, bf16[768,128]{1,0:T(8,128)(2,1)S(1)}, u32[]{:S(2)}) copy-start(bf16[768,128]{1,0:T(8,128)(2,1)S(1)} %collective-permute-done.9.refs_1_) | copy-start | bytes 589828
  116.5 0.7 copy-start.18
  116.5 0.8 copy-start.4
  116.5 0.9 copy-start.13
  117.4 0.7 copy-start.14
  145.1 41.8 %all-to-all-start.3 = ((bf16[32,112,128]{2,1,0:T(8,128)(2,1)}), bf16[32,112,128]{2,1,0:T(8,128)(2,1)S(1)}, u32[]{:S(2)}, u32[]{:S(2)}) async-start(bf16[32,112,128]{2,1,0:T(8,128)(2,1)} %bitcast.16), calls=%async_computation.3 | async-start | bytes 1835008 | tf_op jit(solution)/shard_map/all_to_all | solution.py:284

commit v3 on v2

--- a/solution.py
+++ b/solution.py
@@ -271,7 +271,7 @@
     limit = jnp.where(first_column, text_len[0], 0).astype(jnp.int32)[None]
     held = after(held, queries[0], queries[2])
     packed = attend_text(limit, held, [own[0], own[2], both])
-    edges = after(own[4], left[1], right[1])
+    edges = after(own[4], left[1], right[1], queries[1], queries[3])
     left[4], right[4] = send(edges, to_width(1)), send(edges, to_width(-1))
     packed = lax.all_to_all(packed.reshape(16, 16, 256), GROUP, 0, 0, tiled=True)
 

time: 191 us -> 192 us (level)
  the two profiles are of different devices: /device:TPU:8 before, /device:TPU:12 now
where the time goes in v3:
time: 192 us; the launch traced here: 191 us
  starting transfers between devices  76 us (40%)
  waiting for transfers between devices  68.1 us (35%)
  Pallas kernels  23.2 us (12%)
  local copies, waits for them, and re-layouts  13.6 us (7%)
  blocking collectives  6.47 us (3%)
  between operations  1.95 us (1%)
    ppermute x17, starting transfers between devices, send(): return lax.ppermute(value, NAMES, pairs_of(target))  49.8 us
    ppermute x17, waiting for transfers between devices, send(): return lax.ppermute(value, NAMES, pairs_of(target))  34.9 us
    all_to_all x1, waiting for transfers between devices, shards(): lax.all_to_all(done.reshape(32, CHUNK, HEAD), ('zp', 'zr', 'yh'), 0, 0, t...  33.2 us
    pallas_call x1, Pallas kernels, attend_column(): pl.pallas_call(column_kernel, out_shape=jax.ShapeDtypeStruct((2, 4, 4, CH...  19.4 us
    all_to_all x1, starting transfers between devices, shards(): lax.all_to_all(done.reshape(32, CHUNK, HEAD), ('zp', 'zr', 'yh'), 0, 0, t...  10.6 us
    all_to_all x1, starting transfers between devices, shards(): lax.all_to_all(jnp.broadcast_to(held, (16, 3, 16, HEAD)), GROUP, 0, 0, ti...  9.75 us
    all_to_all x1, blocking collectives, shards(): done = lax.all_to_all(done, 'c', 0, 0, tiled=True)  6.47 us
    all_to_all x1, starting transfers between devices, shards(): lax.all_to_all(packed.reshape(16, 16, 256), GROUP, 0, 0, tiled=True)  5.85 us
  transfers between devices with their start and end apart: 20, of which 5 were waited for; matrix products, arithmetic and copies ran while one was open for 4% of the time, Pallas kernels for 2%

profile of v3, /device:TPU:12, one launch (start us, length us, event | category | flops | bytes accessed | tf_op | source)
XLA Modules:
  0.0 191.2 jit_solution(8488271413881532560)
XLA Ops:
  0.7 0.7 copy-done.19
  1.4 0.1 reshape.42
  1.5 0.0 copy-start.17
  1.5 0.0 copy-start.16
  1.5 0.6 copy-done.18
  2.2 0.0 copy-done.17
  2.2 0.0 copy-done.16
  2.2 1.6 constant_dynamic-slice_fusion.16
  3.9 6.1 %collective-permute-start.2 = (bf16[1552,128]{1,0:T(8,128)(2,1)S(1)}, bf16[1552,128]{1,0:T(8,128)(2,1)S(1)}, u32[]{:S(2)}, u32[]{:S(2)}) collective-permute-start(bf16[1552,128]{1,0:T(8,128)(2,1)S(1)} %pad_maximum_fusion.2), channel_id=1, source_target_pairs={{0,64},{1,192},{2,66},{3,194},{4,68},{5,196},{6,70},{7,198},{8,72}... | collective-permute-start | bytes 1191944 | tf_op jit(solution)/shard_map/ppermute | solution.py:41
  10.0 0.7 collective-permute-start
  10.8 16.6 %collective-permute-done.2.refs_1_.refs_5_ = bf16[1552,128]{1,0:T(8,128)(2,1)S(1)} collective-permute-done((bf16[1552,128]{1,0:T(8,128)(2,1)S(1)}, bf16[1552,128]{1,0:T(8,128)(2,1)S(1)}, u32[]{:S(2)}, u32[]{:S(2)}) %collective-permute-start.2) | collective-permute-done | bytes 397344 | tf_op jit(solution)/shard_map/ppermute | solution.py:41
  27.4 1.3 collective-permute-start.3
  28.7 2.2 %collective-permute-start.1 = (bf16[1552,128]{1,0:T(8,128)(2,1)S(1)}, bf16[1552,128]{1,0:T(8,128)(2,1)S(1)}, u32[]{:S(2)}, u32[]{:S(2)}) collective-permute-start(bf16[1552,128]{1,0:T(8,128)(2,1)S(1)} %pad_maximum_fusion.1), channel_id=1, source_target_pairs={{0,32},{1,160},{2,34},{3,162},{4,36},{5,164},{6,38},{7,166},{8,40}... | collective-permute-start | bytes 1191944 | tf_op jit(solution)/shard_map/ppermute | solution.py:41
  31.6 2.4 %collective-permute-start.8 = (bf16[1552,128]{1,0:T(8,128)(2,1)S(1)}, bf16[1552,128]{1,0:T(8,128)(2,1)S(1)}, u32[]{:S(2)}, u32[]{:S(2)}) collective-permute-start(bf16[1552,128]{1,0:T(8,128)(2,1)S(1)} %collective-permute-done.2.refs_1_.refs_5_), channel_id=1, source_target_pairs={{1,24},{3,26},{5,28},{7,30},{8,0},{9,1},{10,2},{11,3},{12,4},{13,5... | collective-permute-start | bytes 1191944 | tf_op jit(solution)/shard_map/ppermute | solution.py:41
  34.1 3.4 %collective-permute-start.4 = (bf16[1552,128]{1,0:T(8,128)(2,1)S(1)}, bf16[1552,128]{1,0:T(8,128)(2,1)S(1)}, u32[]{:S(2)}, u32[]{:S(2)}) collective-permute-start(bf16[1552,128]{1,0:T(8,128)(2,1)S(1)} %collective-permute-done.2.refs_1_.refs_5_), channel_id=1, source_target_pairs={{0,8},{1,9},{2,10},{3,11},{4,12},{5,13},{6,14},{7,15},{8,16},{9,17... | collective-permute-start | bytes 1191944 | tf_op jit(solution)/shard_map/ppermute | solution.py:41
  37.5 2.4 %collective-permute-start.7 = (bf16[1552,128]{1,0:T(8,128)(2,1)S(1)}, bf16[1552,128]{1,0:T(8,128)(2,1)S(1)}, u32[]{:S(2)}, u32[]{:S(2)}) collective-permute-start(bf16[1552,128]{1,0:T(8,128)(2,1)S(1)} %collective-permute-done.refs_0_.refs_4_), channel_id=1, source_target_pairs={{1,24},{3,26},{5,28},{7,30},{8,0},{9,1},{10,2},{11,3},{12,4},{13,5... | collective-permute-start | bytes 1191944 | tf_op jit(solution)/shard_map/ppermute | solution.py:41
  39.9 7.4 %collective-permute-start.6 = (bf16[1552,128]{1,0:T(8,128)(2,1)S(1)}, bf16[1552,128]{1,0:T(8,128)(2,1)S(1)}, u32[]{:S(2)}, u32[]{:S(2)}) collective-permute-start(bf16[1552,128]{1,0:T(8,128)(2,1)S(1)} %collective-permute-done.refs_0_.refs_4_), channel_id=1, source_target_pairs={{0,8},{1,9},{2,10},{3,11},{4,12},{5,13},{6,14},{7,15},{8,16},{9,17... | collective-permute-start | bytes 1191944 | tf_op jit(solution)/shard_map/ppermute | solution.py:41
  47.4 0.0 copy-start.7
  47.4 1.0 select_select_fusion
  48.4 0.1 constant_dynamic-update-slice_fusion.8.refs_2_.refs_6_
  48.5 2.1 %collective-permute-start.14 = (bf16[3104,128]{1,0:T(8,128)(2,1)S(1)}, bf16[3104,128]{1,0:T(8,128)(2,1)S(1)}, u32[]{:S(2)}, u32[]{:S(2)}) collective-permute-start(bf16[3104,128]{1,0:T(8,128)(2,1)S(1)} %constant_dynamic-update-slice_fusion.8.refs_2_.refs_6_), channel_id=1, source_target_pairs={{1,24},{3,26},{5,28},{7,30},{8,0},{9,1},{10,2},{11,3},{12,4},{13,5... | collective-permute-start | bytes 2383880 | tf_op jit(solution)/shard_map/ppermute | solution.py:41
  50.5 0.7 constant_dynamic-update-slice_fusion.6
  51.2 0.7 constant_dynamic-update-slice_fusion.2
  51.9 0.0 collective-permute-done.8.refs_13_
  52.0 5.3 %collective-permute-start.13 = (bf16[3104,128]{1,0:T(8,128)(2,1)S(1)}, bf16[3104,128]{1,0:T(8,128)(2,1)}, u32[]{:S(2)}, u32[]{:S(2)}) collective-permute-start(bf16[3104,128]{1,0:T(8,128)(2,1)S(1)} %constant_dynamic-update-slice_fusion.8.refs_2_.refs_6_), channel_id=1, source_target_pairs={{0,8},{1,9},{2,10},{3,11},{4,12},{5,13},{6,14},{7,15},{8,16},{9,17... | collective-permute-start | bytes 2383880 | tf_op jit(solution)/shard_map/ppermute | solution.py:41
  57.3 0.0 collective-permute-done.7.refs_12_
  57.3 0.0 collective-permute-done.6.refs_8_
  57.4 0.7 copy-done.9
  58.1 0.2 copy-done.10
  58.2 0.2 copy-done.11
  58.4 0.7 broadcast_in_dim.6
  59.1 9.8 %all-to-all-start = ((bf16[16,3,16,128]{3,2,1,0:T(8,128)(2,1)}), bf16[16,3,16,128]{3,2,1,0:T(8,128)(2,1)S(1)}, u32[]{:S(2)}, u32[]{:S(2)}) async-start(bf16[16,3,16,128]{3,2,1,0:T(8,128)(2,1)} %broadcast_in_dim.6), calls=%async_computation | async-start | bytes 393216 | tf_op jit(solution)/shard_map/all_to_all | solution.py:258
  68.8 0.7 pad_add_fusion.params
  69.5 0.9 constant_dynamic-slice_fusion.1
  70.4 3.0 %collective-permute-start.5 = (bf16[768,128]{1,0:T(8,128)(2,1)}, bf16[768,128]{1,0:T(8,128)(2,1)}, u32[]{:S(2)}, u32[]{:S(2)}) collective-permute-start(bf16[768,128]{1,0:T(8,128)(2,1)} %get-tuple-element.13), channel_id=1, source_target_pairs={{0,0},{1,128},{2,2},{3,130},{4,4},{5,132},{6,6},{7,134},{8,8},{9,1... | collective-permute-start | bytes 589832 | tf_op jit(solution)/shard_map/ppermute | solution.py:41
  73.4 1.9 collective-permute-start.10
  75.3 2.4 %collective-permute-start.12 = (bf16[1552,128]{1,0:T(8,128)(2,1)}, bf16[1552,128]{1,0:T(8,128)(2,1)S(1)}, u32[]{:S(2)}, u32[]{:S(2)}) collective-permute-start(bf16[1552,128]{1,0:T(8,128)(2,1)} %get-tuple-element.32), channel_id=1, source_target_pairs={{0,256},{1,257},{2,258},{3,259},{4,260},{5,261},{6,262},{7,263},{8... | collective-permute-start | bytes 1191944 | tf_op jit(solution)/shard_map/ppermute | solution.py:41
  77.8 0.7 copy.19
  78.5 10.9 %collective-permute-done.10.refs_2_ = bf16[768,128]{1,0:T(8,128)(2,1)} collective-permute-done((bf16[768,128]{1,0:T(8,128)(2,1)}, bf16[768,128]{1,0:T(8,128)(2,1)}, u32[]{:S(2)}, u32[]{:S(2)}) %collective-permute-start.10) | collective-permute-done | bytes 196640 | tf_op jit(solution)/shard_map/ppermute | solution.py:41
  89.4 1.9 collective-permute-start.9
  91.3 1.3 collective-permute-start.11
  92.6 3.8 %attend_text.1 = f32[256,256]{1,0:T(8,128)} custom-call(s32[1]{0:T(128)} %bitcast.14.limit, bf16[3,256,128]{2,1,0:T(8,128)(2,1)} %bitcast.49, bf16[1552,128]{1,0:T(8,128)(2,1)} %copy-done.2, bf16[1552,128]{1,0:T(8,128)(2,1)} %copy-done.1, bf16[3104,128]{1,0:T(8,128)(2,1)} %copy-done), custom_call_target="tpu_custom_call" | custom-call | flops 1048576 | bytes 65536 | tf_op jit(solution)/shard_map/attend_text/pallas_call | solution.py:206
  96.4 5.9 %all-to-all-start.1 = ((f32[16,16,256]{2,1,0:T(8,128)}), f32[16,16,256]{2,1,0:T(8,128)S(1)}, u32[]{:S(2)}, u32[]{:S(2)}) async-start(f32[16,16,256]{2,1,0:T(8,128)} %bitcast.51), calls=%async_computation.1 | async-start | bytes 524288 | tf_op jit(solution)/shard_map/all_to_all | solution.py:276
  102.3 0.7 slice_bitcast_fusion.3
  102.9 0.0 collective-permute-done.12.refs_7_
  102.9 0.0 collective-permute-done.9.refs_1_
  103.0 0.0 collective-permute-done.14.refs_14_
  103.0 2.5 %collective-permute-start.16 = (bf16[1552,128]{1,0:T(8,128)(2,1)S(1)}, bf16[1552,128]{1,0:T(8,128)(2,1)S(1)}, u32[]{:S(2)}, u32[]{:S(2)}) collective-permute-start(bf16[1552,128]{1,0:T(8,128)(2,1)S(1)} %collective-permute-done.12.refs_7_), channel_id=1, source_target_pairs={{1,24},{3,26},{5,28},{7,30},{8,0},{9,1},{10,2},{11,3},{12,4},{13,5... | collective-permute-start | bytes 1191944 | tf_op jit(solution)/shard_map/ppermute | solution.py:41
  105.5 3.6 %collective-permute-start.15 = (bf16[1552,128]{1,0:T(8,128)(2,1)S(1)}, bf16[1552,128]{1,0:T(8,128)(2,1)S(1)}, u32[]{:S(2)}, u32[]{:S(2)}) collective-permute-start(bf16[1552,128]{1,0:T(8,128)(2,1)S(1)} %collective-permute-done.12.refs_7_), channel_id=1, source_target_pairs={{0,8},{1,9},{2,10},{3,11},{4,12},{5,13},{6,14},{7,15},{8,16},{9,17... | collective-permute-start | bytes 1191944 | tf_op jit(solution)/shard_map/ppermute | solution.py:41
  109.0 0.7 slice_bitcast_fusion.2
  109.8 0.6 reshape.52.lists
  110.4 0.7 slice.26.refs_16_
  111.0 5.1 %collective-permute-done.16.refs_15_ = bf16[1552,128]{1,0:T(8,128)(2,1)S(1)} collective-permute-done((bf16[1552,128]{1,0:T(8,128)(2,1)S(1)}, bf16[1552,128]{1,0:T(8,128)(2,1)S(1)}, u32[]{:S(2)}, u32[]{:S(2)}) %collective-permute-start.16) | collective-permute-done | bytes 397344 | tf_op jit(solution)/shard_map/ppermute | solution.py:41
  116.1 2.2 %collective-permute-done.15.refs_11_ = bf16[1552,128]{1,0:T(8,128)(2,1)S(1)} collective-permute-done((bf16[1552,128]{1,0:T(8,128)(2,1)S(1)}, bf16[1552,128]{1,0:T(8,128)(2,1)S(1)}, u32[]{:S(2)}, u32[]{:S(2)}) %collective-permute-start.15) | collective-permute-done | bytes 397344 | tf_op jit(solution)/shard_map/ppermute | solution.py:41
  118.4 0.0 copy-start.14
  118.4 0.7 copy-done.14
  119.1 19.4 %attend_column.1 = bf16[2,4,4,112,128]{4,3,2,1,0:T(8,128)(2,1)} custom-call(s32[4]{0:T(128)} %pad_add_fusion.params, s32[64]{0:T(128)} %reshape.52.lists, bf16[768,128]{1,0:T(8,128)(2,1)} %collective-permute-done.5.refs_0_, bf16[768,128]{1,0:T(8,128)(2,1)} %collective-permute-done.9.refs_1_, bf16[768,128]{1,0:T(8,128)(2,1)} %collective-permute-done.10.refs_2_, ...), custom_call_target="tpu_custom_call" | custom-call | flops 1048576 | bytes 65536 | tf_op jit(solution)/shard_map/attend_column/pallas_call | solution.py:155
  138.5 6.5 %all_to_all.20 = bf16[2,4,4,112,128]{4,3,2,1,0:T(8,128)(2,1)} all-to-all(bf16[2,4,4,112,128]{4,3,2,1,0:T(8,128)(2,1)} %attend_column.1), channel_id=1, replica_groups=mesh['yl'=2,'zr'=4,'zp'=2,'x'=4,'yh'=4,'c'=2] {'c'}, dimensions={0} | all-to-all | bytes 1835008 | tf_op jit(solution)/shard_map/all_to_all | solution.py:283
  145.0 10.6 %all-to-all-start.3 = ((bf16[32,112,128]{2,1,0:T(8,128)(2,1)}), bf16[32,112,128]{2,1,0:T(8,128)(2,1)S(1)}, u32[]{:S(2)}, u32[]{:S(2)}) async-start(bf16[32,112,128]{2,1,0:T(8,128)(2,1)} %bitcast.16), calls=%async_computation.3 | async-start | bytes 1835008 | tf_op jit(solution)/shard_map/all_to_all | solution.py:284
  155.6 33.2 %all-to-all-done.3 = bf16[32,112,128]{2,1,0:T(8,128)(2,1)S(1)} async-done(((bf16[32,112,128]{2,1,0:T(8,128)(2,1)}), bf16[32,112,128]{2,1,0:T(8,128)(2,1)S(1)}, u32[]{:S(2)}, u32[]{:S(2)}) %all-to-all-start.3) | async-done | bytes 917536 | tf_op jit(solution)/shard_map/all_to_all | solution.py:284
  188.8 0.1 copy.20
  189.0 0.4 copy.21
  189.4 1.2 reshape.50
  190.6 0.6 fusion
  (59 shorter events, 0.4 us)
Async XLA Ops:
  0.7 0.7 copy-start.19
  1.5 0.7 copy-start.18
  1.5 0.7 copy-start.17
  1.5 0.7 copy-start.16
  3.9 23.5 %collective-permute-start.2 = (bf16[1552,128]{1,0:T(8,128)(2,1)S(1)}, bf16[1552,128]{1,0:T(8,128)(2,1)S(1)}, u32[]{:S(2)}, u32[]{:S(2)}) collective-permute-start(bf16[1552,128]{1,0:T(8,128)(2,1)S(1)} %pad_maximum_fusion.2), channel_id=1, source_target_pairs={{0,64},{1,192},{2,66},{3,194},{4,68},{5,196},{6,70},{7,198},{8,72}... | collective-permute-start | bytes 1191944 | tf_op jit(solution)/shard_map/ppermute | solution.py:41
  10.0 18.7 %collective-permute-start = (bf16[1552,128]{1,0:T(8,128)(2,1)S(1)}, bf16[1552,128]{1,0:T(8,128)(2,1)S(1)}, u32[]{:S(2)}, u32[]{:S(2)}) collective-permute-start(bf16[1552,128]{1,0:T(8,128)(2,1)S(1)} %pad_maximum_fusion), channel_id=1, source_target_pairs={{0,0},{1,128},{2,2},{3,130},{4,4},{5,132},{6,6},{7,134},{8,8},{9,1... | collective-permute-start | bytes 1191944 | tf_op jit(solution)/shard_map/ppermute | solution.py:41
  27.4 50.3 %copy-start.1 = (bf16[1552,128]{1,0:T(8,128)(2,1)}, bf16[1552,128]{1,0:T(8,128)(2,1)S(1)}, u32[]{:S(2)}) copy-start(bf16[1552,128]{1,0:T(8,128)(2,1)S(1)} %collective-permute-done.2.refs_1_.refs_5_) | copy-start | bytes 1191940
  27.4 12.5 %collective-permute-start.3 = (bf16[1552,128]{1,0:T(8,128)(2,1)S(1)}, bf16[1552,128]{1,0:T(8,128)(2,1)S(1)}, u32[]{:S(2)}, u32[]{:S(2)}) collective-permute-start(bf16[1552,128]{1,0:T(8,128)(2,1)S(1)} %pad_maximum_fusion.3), channel_id=1, source_target_pairs={{64,64},{65,192},{66,66},{67,194},{68,68},{69,196},{70,70},{71,198... | collective-permute-start | bytes 1191944 | tf_op jit(solution)/shard_map/ppermute | solution.py:41
  28.7 22.5 %copy-start.2 = (bf16[1552,128]{1,0:T(8,128)(2,1)}, bf16[1552,128]{1,0:T(8,128)(2,1)S(1)}, u32[]{:S(2)}) copy-start(bf16[1552,128]{1,0:T(8,128)(2,1)S(1)} %collective-permute-done.refs_0_.refs_4_) | copy-start | bytes 1191940
  28.7 18.7 %collective-permute-start.1 = (bf16[1552,128]{1,0:T(8,128)(2,1)S(1)}, bf16[1552,128]{1,0:T(8,128)(2,1)S(1)}, u32[]{:S(2)}, u32[]{:S(2)}) collective-permute-start(bf16[1552,128]{1,0:T(8,128)(2,1)S(1)} %pad_maximum_fusion.1), channel_id=1, source_target_pairs={{0,32},{1,160},{2,34},{3,162},{4,36},{5,164},{6,38},{7,166},{8,40}... | collective-permute-start | bytes 1191944 | tf_op jit(solution)/shard_map/ppermute | solution.py:41
  31.6 20.3 %collective-permute-start.8 = (bf16[1552,128]{1,0:T(8,128)(2,1)S(1)}, bf16[1552,128]{1,0:T(8,128)(2,1)S(1)}, u32[]{:S(2)}, u32[]{:S(2)}) collective-permute-start(bf16[1552,128]{1,0:T(8,128)(2,1)S(1)} %collective-permute-done.2.refs_1_.refs_5_), channel_id=1, source_target_pairs={{1,24},{3,26},{5,28},{7,30},{8,0},{9,1},{10,2},{11,3},{12,4},{13,5... | collective-permute-start | bytes 1191944 | tf_op jit(solution)/shard_map/ppermute | solution.py:41
  34.1 23.2 %collective-permute-start.4 = (bf16[1552,128]{1,0:T(8,128)(2,1)S(1)}, bf16[1552,128]{1,0:T(8,128)(2,1)S(1)}, u32[]{:S(2)}, u32[]{:S(2)}) collective-permute-start(bf16[1552,128]{1,0:T(8,128)(2,1)S(1)} %collective-permute-done.2.refs_1_.refs_5_), channel_id=1, source_target_pairs={{0,8},{1,9},{2,10},{3,11},{4,12},{5,13},{6,14},{7,15},{8,16},{9,17... | collective-permute-start | bytes 1191944 | tf_op jit(solution)/shard_map/ppermute | solution.py:41
  37.5 19.8 %collective-permute-start.7 = (bf16[1552,128]{1,0:T(8,128)(2,1)S(1)}, bf16[1552,128]{1,0:T(8,128)(2,1)S(1)}, u32[]{:S(2)}, u32[]{:S(2)}) collective-permute-start(bf16[1552,128]{1,0:T(8,128)(2,1)S(1)} %collective-permute-done.refs_0_.refs_4_), channel_id=1, source_target_pairs={{1,24},{3,26},{5,28},{7,30},{8,0},{9,1},{10,2},{11,3},{12,4},{13,5... | collective-permute-start | bytes 1191944 | tf_op jit(solution)/shard_map/ppermute | solution.py:41
  39.9 17.4 %collective-permute-start.6 = (bf16[1552,128]{1,0:T(8,128)(2,1)S(1)}, bf16[1552,128]{1,0:T(8,128)(2,1)S(1)}, u32[]{:S(2)}, u32[]{:S(2)}) collective-permute-start(bf16[1552,128]{1,0:T(8,128)(2,1)S(1)} %collective-permute-done.refs_0_.refs_4_), channel_id=1, source_target_pairs={{0,8},{1,9},{2,10},{3,11},{4,12},{5,13},{6,14},{7,15},{8,16},{9,17... | collective-permute-start | bytes 1191944 | tf_op jit(solution)/shard_map/ppermute | solution.py:41
  47.4 1.0 copy-start.7
  48.4 21.1 %copy-start.5 = (bf16[768,384]{1,0:T(8,128)(2,1)S(1)}, bf16[768,384]{1,0:T(8,128)(2,1)}, u32[]{:S(2)}) copy-start(bf16[768,384]{1,0:T(8,128)(2,1)} %param.8) | copy-start | bytes 1769476
  48.4 21.9 %copy-start = (bf16[3104,128]{1,0:T(8,128)(2,1)}, bf16[3104,128]{1,0:T(8,128)(2,1)S(1)}, u32[]{:S(2)}) copy-start(bf16[3104,128]{1,0:T(8,128)(2,1)S(1)} %constant_dynamic-update-slice_fusion.8.refs_2_.refs_6_) | copy-start | bytes 2383876
  48.5 54.5 %collective-permute-start.14 = (bf16[3104,128]{1,0:T(8,128)(2,1)S(1)}, bf16[3104,128]{1,0:T(8,128)(2,1)S(1)}, u32[]{:S(2)}, u32[]{:S(2)}) collective-permute-start(bf16[3104,128]{1,0:T(8,128)(2,1)S(1)} %constant_dynamic-update-slice_fusion.8.refs_2_.refs_6_), channel_id=1, source_target_pairs={{1,24},{3,26},{5,28},{7,30},{8,0},{9,1},{10,2},{11,3},{12,4},{13,5... | collective-permute-start | bytes 2383880 | tf_op jit(solution)/shard_map/ppermute | solution.py:41
  52.0 5.4 %copy-start.8 = (bf16[1552,128]{1,0:T(8,128)(2,1)}, bf16[1552,128]{1,0:T(8,128)(2,1)S(1)}, u32[]{:S(2)}) copy-start(bf16[1552,128]{1,0:T(8,128)(2,1)S(1)} %collective-permute-done.8.refs_13_) | copy-start | bytes 1191940
  52.0 51.0 %collective-permute-start.13 = (bf16[3104,128]{1,0:T(8,128)(2,1)S(1)}, bf16[3104,128]{1,0:T(8,128)(2,1)}, u32[]{:S(2)}, u32[]{:S(2)}) collective-permute-start(bf16[3104,128]{1,0:T(8,128)(2,1)S(1)} %constant_dynamic-update-slice_fusion.8.refs_2_.refs_6_), channel_id=1, source_target_pairs={{0,8},{1,9},{2,10},{3,11},{4,12},{5,13},{6,14},{7,15},{8,16},{9,17... | collective-permute-start | bytes 2383880 | tf_op jit(solution)/shard_map/ppermute | solution.py:41
  57.3 0.8 copy-start.9
  57.3 0.9 copy-start.10
  57.3 1.0 copy-start.11
  59.1 18.6 %all-to-all-start = ((bf16[16,3,16,128]{3,2,1,0:T(8,128)(2,1)}), bf16[16,3,16,128]{3,2,1,0:T(8,128)(2,1)S(1)}, u32[]{:S(2)}, u32[]{:S(2)}) async-start(bf16[16,3,16,128]{3,2,1,0:T(8,128)(2,1)} %broadcast_in_dim.6), calls=%async_computation | async-start | bytes 393216 | tf_op jit(solution)/shard_map/all_to_all | solution.py:258
  70.4 8.1 %collective-permute-start.5 = (bf16[768,128]{1,0:T(8,128)(2,1)}, bf16[768,128]{1,0:T(8,128)(2,1)}, u32[]{:S(2)}, u32[]{:S(2)}) collective-permute-start(bf16[768,128]{1,0:T(8,128)(2,1)} %get-tuple-element.13), channel_id=1, source_target_pairs={{0,0},{1,128},{2,2},{3,130},{4,4},{5,132},{6,6},{7,134},{8,8},{9,1... | collective-permute-start | bytes 589832 | tf_op jit(solution)/shard_map/ppermute | solution.py:41
  73.4 16.0 %collective-permute-start.10 = (bf16[768,128]{1,0:T(8,128)(2,1)}, bf16[768,128]{1,0:T(8,128)(2,1)}, u32[]{:S(2)}, u32[]{:S(2)}) collective-permute-start(bf16[768,128]{1,0:T(8,128)(2,1)} %get-tuple-element.16), channel_id=1, source_target_pairs={{0,64},{1,192},{2,66},{3,194},{4,68},{5,196},{6,70},{7,198},{8,72}... | collective-permute-start | bytes 589832 | tf_op jit(solution)/shard_map/ppermute | solution.py:41
  75.3 27.7 %collective-permute-start.12 = (bf16[1552,128]{1,0:T(8,128)(2,1)}, bf16[1552,128]{1,0:T(8,128)(2,1)S(1)}, u32[]{:S(2)}, u32[]{:S(2)}) collective-permute-start(bf16[1552,128]{1,0:T(8,128)(2,1)} %get-tuple-element.32), channel_id=1, source_target_pairs={{0,256},{1,257},{2,258},{3,259},{4,260},{5,261},{6,262},{7,263},{8... | collective-permute-start | bytes 1191944 | tf_op jit(solution)/shard_map/ppermute | solution.py:41
  77.7 11.6 %copy-start.15 = (bf16[768,128]{1,0:T(8,128)(2,1)S(1)}, bf16[768,128]{1,0:T(8,128)(2,1)}, u32[]{:S(2)}) copy-start(bf16[768,128]{1,0:T(8,128)(2,1)} %get-tuple-element.15) | copy-start | bytes 589828
  89.4 13.6 %collective-permute-start.9 = (bf16[768,128]{1,0:T(8,128)(2,1)S(1)}, bf16[768,128]{1,0:T(8,128)(2,1)}, u32[]{:S(2)}, u32[]{:S(2)}) collective-permute-start(bf16[768,128]{1,0:T(8,128)(2,1)S(1)} %copy-done.15), channel_id=1, source_target_pairs={{0,32},{1,160},{2,34},{3,162},{4,36},{5,164},{6,38},{7,166},{8,40}... | collective-permute-start | bytes 589832 | tf_op jit(solution)/shard_map/ppermute | solution.py:41
  91.3 11.7 %collective-permute-start.11 = (bf16[768,128]{1,0:T(8,128)(2,1)S(1)}, bf16[768,128]{1,0:T(8,128)(2,1)}, u32[]{:S(2)}, u32[]{:S(2)}) collective-permute-start(bf16[768,128]{1,0:T(8,128)(2,1)S(1)} %get-tuple-element.17), channel_id=1, source_target_pairs={{64,64},{65,192},{66,66},{67,194},{68,68},{69,196},{70,70},{71,198... | collective-permute-start | bytes 589832 | tf_op jit(solution)/shard_map/ppermute | solution.py:41
  96.4 13.9 %copy-start.3 = (bf16[3,16,16,128]{3,2,1,0:T(8,128)(2,1)S(1)}, bf16[3,16,16,128]{3,2,1,0:T(8,128)(2,1)}, u32[]{:S(2)}) copy-start(bf16[3,16,16,128]{3,2,1,0:T(8,128)(2,1)} %copy.19) | copy-start | bytes 589828
  96.4 14.6 %all-to-all-start.1 = ((f32[16,16,256]{2,1,0:T(8,128)}), f32[16,16,256]{2,1,0:T(8,128)S(1)}, u32[]{:S(2)}, u32[]{:S(2)}) async-start(f32[16,16,256]{2,1,0:T(8,128)} %bitcast.51), calls=%async_computation.1 | async-start | bytes 524288 | tf_op jit(solution)/shard_map/all_to_all | solution.py:276
  102.9 15.4 %copy-start.12 = (bf16[1552,128]{1,0:T(8,128)(2,1)}, bf16[1552,128]{1,0:T(8,128)(2,1)S(1)}, u32[]{:S(2)}) copy-start(bf16[1552,128]{1,0:T(8,128)(2,1)S(1)} %collective-permute-done.12.refs_7_) | copy-start | bytes 1191940
  103.0 15.4 %copy-start.6 = (bf16[3104,128]{1,0:T(8,128)(2,1)}, bf16[3104,128]{1,0:T(8,128)(2,1)S(1)}, u32[]{:S(2)}) copy-start(bf16[3104,128]{1,0:T(8,128)(2,1)S(1)} %collective-permute-done.14.refs_14_) | copy-start | bytes 2383876
  103.0 13.2 %collective-permute-start.16 = (bf16[1552,128]{1,0:T(8,128)(2,1)S(1)}, bf16[1552,128]{1,0:T(8,128)(2,1)S(1)}, u32[]{:S(2)}, u32[]{:S(2)}) collective-permute-start(bf16[1552,128]{1,0:T(8,128)(2,1)S(1)} %collective-permute-done.12.refs_7_), channel_id=1, source_target_pairs={{1,24},{3,26},{5,28},{7,30},{8,0},{9,1},{10,2},{11,3},{12,4},{13,5... | collective-permute-start | bytes 1191944 | tf_op jit(solution)/shard_map/ppermute | solution.py:41
  105.5 12.9 %collective-permute-start.15 = (bf16[1552,128]{1,0:T(8,128)(2,1)S(1)}, bf16[1552,128]{1,0:T(8,128)(2,1)S(1)}, u32[]{:S(2)}, u32[]{:S(2)}) collective-permute-start(bf16[1552,128]{1,0:T(8,128)(2,1)S(1)} %collective-permute-done.12.refs_7_), channel_id=1, source_target_pairs={{0,8},{1,9},{2,10},{3,11},{4,12},{5,13},{6,14},{7,15},{8,16},{9,17... | collective-permute-start | bytes 1191944 | tf_op jit(solution)/shard_map/ppermute | solution.py:41
  111.0 7.3 %copy-start.4 = (f32[16,16,256]{2,1,0:T(8,128)}, f32[16,16,256]{2,1,0:T(8,128)S(1)}, u32[]{:S(2)}) copy-start(f32[16,16,256]{2,1,0:T(8,128)S(1)} %all-to-all-done.1.refs_17_) | copy-start | bytes 786436
  116.1 2.2 %copy-start.13 = (bf16[1552,128]{1,0:T(8,128)(2,1)}, bf16[1552,128]{1,0:T(8,128)(2,1)S(1)}, u32[]{:S(2)}) copy-start(bf16[1552,128]{1,0:T(8,128)(2,1)S(1)} %collective-permute-done.16.refs_15_) | copy-start | bytes 1191940
  118.4 0.8 copy-start.14
  145.0 43.8 %all-to-all-start.3 = ((bf16[32,112,128]{2,1,0:T(8,128)(2,1)}), bf16[32,112,128]{2,1,0:T(8,128)(2,1)S(1)}, u32[]{:S(2)}, u32[]{:S(2)}) async-start(bf16[32,112,128]{2,1,0:T(8,128)(2,1)} %bitcast.16), calls=%async_computation.3 | async-start | bytes 1835008 | tf_op jit(solution)/shard_map/all_to_all | solution.py:284
